TPU v7x, 128 devices: a whole 4x4x4 slice. The times are simulated.
128 devices in a mesh: row: 8 (over x_lo, z), col: 16 (over x_hi, y, core).
Axes of the slice: x: 4 (x_hi: 2, x_lo: 2; x = x_hi * 2 + x_lo), y: 4, z: 4, core: 2. Of those that a mesh axis runs over, the one named last changes fastest.
Arguments:
- pair_tensor: float32 [768, 768, 128], P(('row', 'col')), may hold values from -30 to 30
- token_mask: int32 [768], replicated, may hold values from 0 to 1, as said below
- ln_gain: float32 [2, 128], replicated, may hold values from 0.5 to 1.5
- ln_shift: float32 [2, 128], replicated, may hold values from -3 to 3
- w_query: float32 [2, 128, 128], replicated, may hold values from -5 to 5
- w_key: float32 [2, 128, 128], replicated, may hold values from -5 to 5
- w_value: float32 [2, 128, 128], replicated, may hold values from -0.5 to 0.5
- w_bias: float32 [2, 4, 128], replicated, may hold values from -0.5 to 0.5
- w_gate: float32 [2, 128, 128], replicated, may hold values from -0.5 to 0.5
- gate_shift: float32 [2, 128], replicated, may hold values from -4 to 4
- w_out: float32 [2, 128, 128], replicated, may hold values from -0.5 to 0.5
Outputs:
- updated_pair: float32 [768, 768, 128], P(('row', 'col'))
Inputs may be any that keep to these rules, and one draw needn't show every extreme that they name: Real tokens come first: token_mask is 1 on a leading run of tokens and 0 after it; token 0 is real and token 767 is padding.
All inputs are finite; a program needn't handle non-finite values.
Results may differ from a plain program's by a relative error of at most 0.00055.
Values may be sent and summed in bfloat16 or wider, within the bound.
No kernel may reach another device: no remote copies, remote signals or barrier semaphores. Data moves between devices by JAX's collectives and lax.ppermute only.
A program may use at most 128 MiB of HBM per device.

v0:
```python
import functools

import jax
import jax.numpy as jnp
import numpy as np
from jax import lax
from jax.experimental import pallas as pl
from jax.experimental.pallas import tpu as pltpu
from jax.sharding import PartitionSpec as P

HEADS = 4
HEAD_DIM = 32
HD = 128
TOKENS = 768
ROWS = 6
DEVICES = 128
PADDED = 40
EPSILON = 1e-05
NEGATIVE = -1e30
LOG2E = 1.4426950408889634
CURVE = 4.0
CODE_STEP = float(np.log(1 + CURVE * 11.32) / 32767)
AXES = ("row", "col")
VMEM = 60 * 1024 * 1024
F32, BF16 = jnp.float32, jnp.bfloat16
NT = (((1,), (1,)), ((), ()))
NN = (((1,), (0,)), ((), ()))


def coords(device):
    row, col = divmod(device, 16)
    x_lo, z = divmod(row, 4)
    x_hi, rest = divmod(col, 8)
    y, core = divmod(rest, 2)
    return [x_hi * 2 + x_lo, y, z, core]


def device_at(x, y, z, core):
    return ((x % 2) * 4 + z) * 16 + (x // 2) * 8 + y * 2 + core


def shifted(values, axis, step):
    pairs = []
    for source in range(DEVICES):
        place = coords(source)
        place[axis] = (place[axis] + step) % (2 if axis == 3 else 4)
        pairs.append((source, device_at(*place)))
    return lax.ppermute(values, AXES, pairs)


def ring(block, axis):
    return jnp.concatenate(
        [block, shifted(block, axis, 1), shifted(block, axis, 2), shifted(block, axis, -1)], 0
    )


def merge_kernel(scalar_ref, *refs):
    to = lax.broadcasted_iota(jnp.int32, (192, 192), 0)
    of = lax.broadcasted_iota(jnp.int32, (192, 192), 1)
    head, y, core, row = to // 48, (to // 12) % 4, (to // 6) % 2, to % 6
    behind = (scalar_ref[1] - y) & 3
    source = (behind * 2 + (core ^ scalar_ref[3])) * 24 + row * 4 + head
    order = jnp.where(of == source, 1.0, 0.0).astype(BF16)
    slots = jnp.concatenate([ref[...] for ref in refs[:4]], axis=0)
    ordered = dot(order, slots).astype(BF16)
    for head_at in range(HEADS):
        refs[4 + head_at // 2][head_at % 2] = ordered[head_at * 48 : (head_at + 1) * 48]


def merge(scalars, slots):
    vmem = pl.BlockSpec(memory_space=pltpu.VMEM)
    return pl.pallas_call(
        merge_kernel,
        in_specs=[pl.BlockSpec(memory_space=pltpu.SMEM)] + [vmem] * 4,
        out_shape=[jax.ShapeDtypeStruct((2, 48, 384), BF16)] * 2,
        compiler_params=pltpu.CompilerParams(vmem_limit_bytes=VMEM),
        cost_estimate=pl.CostEstimate(flops=10**7, bytes_accessed=3 * 10**5, transcendentals=0),
    )(scalars, *slots)


def gather_plane(place, kept, sent, beside, work):
    block = jnp.concatenate([kept, shifted(sent, 3, 1)], axis=0)
    slots = [block] + [shifted(block, 1, step) for step in (1, 2, -1)]
    blocks = [ring(pair[None], axis) for pair, axis in zip(merge(place, slots), (0, 2))]
    *blocks, beside = lax.optimization_barrier((*blocks, beside))
    blocks = [ring(block, axis) for block, axis in zip(blocks, (2, 0))]
    *blocks, done = lax.optimization_barrier((*blocks, work(beside)))
    pieces = []
    for block in blocks:
        pieces += [block, shifted(block, 3, 1)]
    return pieces, done


def split(values):
    high = values.astype(BF16)
    return high, (values - high.astype(F32)).astype(BF16)


def dot(a, b, dims=NN):
    return lax.dot_general(a, b, dims, preferred_element_type=F32)


def dot3(a, b, dims=NN):
    (a_high, a_low), (b_high, b_low) = a, b
    return dot(a_high, b_high, dims) + (dot(a_low, b_high, dims) + dot(a_high, b_low, dims))


def dot_split(a, b_twice, b_low):
    return dot(a, b_twice) + dot(a[:, :HD], b_low)


def side_by_side(values):
    return jnp.concatenate(split(values), axis=1)


def twice(weight):
    high, low = split(weight)
    return jnp.concatenate([high, high], axis=0), low


def standardize(values):
    mean = jnp.full((2 * HD, HD), 1.0 / HD, BF16)
    centred = values - dot(side_by_side(values), mean)
    spread = dot(side_by_side(centred * centred), mean)
    return centred * lax.rsqrt(spread + EPSILON)


def normalize(values, gain, shift):
    return standardize(values) * gain + shift


def encode(values):
    size = jnp.floor(jnp.log(1.0 + CURVE * jnp.abs(values)) * (1 / CODE_STEP) + 0.5)
    return jnp.where(values < 0, -size, size)


def decode(codes):
    size = (jnp.exp(jnp.abs(codes) * CODE_STEP) - 1.0) * (1 / CURVE)
    return jnp.where(codes < 0, -size, size)


def put_bias(normed, w_bias, rows_ref, row):
    bias = dot3(split(w_bias), split(normed), NT)
    for half in range(2):
        at = half * 24 + row * 4
        rows_ref[at : at + 4, :] = bias[:, half * 384 : (half + 1) * 384]


def hand_over(scalar_ref, rows_ref, kept_ref, sent_ref):
    first, second = rows_ref[:24, :].astype(BF16), rows_ref[24:, :].astype(BF16)
    kept_ref[...] = jnp.where(scalar_ref[3] == 0, first, second)
    sent_ref[...] = jnp.where(scalar_ref[3] == 0, second, first)


def bias_kernel(scalar_ref, x_ref, gain_ref, shift_ref, w_ref, kept_ref, sent_ref, rows_ref):
    for row in range(ROWS):
        normed = normalize(x_ref[row], gain_ref[0:1, :], shift_ref[0:1, :])
        put_bias(normed, w_ref[0], rows_ref, row)
    hand_over(scalar_ref, rows_ref, kept_ref, sent_ref)


def first_bias(scalars, x, gain, shift, w_bias):
    vmem = pl.BlockSpec(memory_space=pltpu.VMEM)
    return pl.pallas_call(
        bias_kernel,
        in_specs=[pl.BlockSpec(memory_space=pltpu.SMEM)] + [vmem] * 4,
        out_shape=[jax.ShapeDtypeStruct((24, 384), BF16)] * 2,
        scratch_shapes=[pltpu.VMEM((48, 384), F32)],
        compiler_params=pltpu.CompilerParams(vmem_limit_bytes=VMEM),
        cost_estimate=pl.CostEstimate(flops=10**8, bytes_accessed=2 * 10**6, transcendentals=0),
    )(scalars, x, gain, shift, w_bias)


def lane_group():
    return lax.broadcasted_iota(jnp.int32, (1, HD), 1) // HEAD_DIM


def spreader(source_of):
    row = lax.broadcasted_iota(jnp.int32, (2 * HD, HEADS * HD), 0)
    column = lax.broadcasted_iota(jnp.int32, (2 * HD, HEADS * HD), 1)
    head, group, d = column // HD, (column // HEAD_DIM) % 4, column % HEAD_DIM
    part = source_of(head, group)
    hit = (part >= 0) & (row == part * HD + head * HEAD_DIM + d)
    return jnp.where(hit, 1.0, 0.0).astype(BF16)


def prepare_weights(weights, w_twice_ref, w_low_ref, spread_ref):
    for at, weight in enumerate(weights):
        high, low = twice(weight)
        w_twice_ref[:, at * HD : (at + 1) * HD] = high
        w_low_ref[:, at * HD : (at + 1) * HD] = low
    spread_ref[0] = spreader(lambda head, group: group % 2)
    spread_ref[1] = spreader(lambda head, group: group // 2)


def project_kernel(
    crossed, x_ref, gain_ref, shift_ref, gs_ref, wq_ref, wk_ref, wv_ref, wg_ref, q_ref, k_ref, v_ref, g_ref,
    w_twice_ref, w_low_ref, spread_ref, *rest,
):
    step = pl.program_id(0)

    @pl.when(step == 0)
    def _():
        weights = [wq_ref[0] * (HEAD_DIM**-0.5 * LOG2E), wk_ref[0], wv_ref[0], wg_ref[0]]
        prepare_weights(weights, w_twice_ref, w_low_ref, spread_ref)

    if crossed:
        for row in range(ROWS):
            rest[0][pl.ds(row, DEVICES, stride=ROWS), :] = x_ref[
                pl.ds(row * ROWS + step, DEVICES, stride=PADDED), :
            ]
        standard = decode(rest[0][...])
    else:
        standard = standardize(x_ref[0])
    own = slice(int(crossed), int(crossed) + 1)
    cells = side_by_side(standard * gain_ref[own, :] + shift_ref[own, :])

    def columns(at):
        cut = slice(at * HD, (at + 1) * HD)
        return dot_split(cells, w_twice_ref[:, cut], w_low_ref[:, cut])

    for at, ref in enumerate((q_ref, k_ref)):
        parts = side_by_side(columns(at))
        for pair in range(2):
            cut = slice(pair * 2 * HD, (pair + 1) * 2 * HD)
            spread = dot(parts, spread_ref[at, :, cut]).astype(BF16)
            ref[0, 2 * pair] = spread[:, :HD]
            ref[0, 2 * pair + 1] = spread[:, HD:]
    v_ref[0] = side_by_side(columns(2))
    g_ref[0] = jax.nn.sigmoid(columns(3) + gs_ref[own, :])


def matrix(second):
    return pl.BlockSpec((1, HD, HD), lambda i: (int(second), 0, 0))


def project(crossed, x, vectors, matrices):
    whole = pl.BlockSpec(memory_space=pltpu.VMEM)
    row_spec = pl.BlockSpec((1, TOKENS, HD), lambda i: (i, 0, 0))
    head_spec = pl.BlockSpec((1, HEADS, TOKENS, HD), lambda i: (i, 0, 0, 0))
    scratch = [
        pltpu.VMEM((2 * HD, 4 * HD), BF16),
        pltpu.VMEM((HD, 4 * HD), BF16),
        pltpu.VMEM((2, 2 * HD, HEADS * HD), BF16),
    ]
    if crossed:
        scratch.append(pltpu.VMEM((TOKENS, HD), F32))
    return pl.pallas_call(
        functools.partial(project_kernel, crossed),
        grid=(ROWS,),
        in_specs=[whole if crossed else row_spec] + [whole] * 3 + [matrix(crossed)] * 4,
        out_specs=[
            head_spec, head_spec, pl.BlockSpec((1, TOKENS, 2 * HD), lambda i: (i, 0, 0)), row_spec,
        ],
        out_shape=[
            jax.ShapeDtypeStruct((ROWS, HEADS, TOKENS, HD), BF16),
            jax.ShapeDtypeStruct((ROWS, HEADS, TOKENS, HD), BF16),
            jax.ShapeDtypeStruct((ROWS, TOKENS, 2 * HD), BF16),
            jax.ShapeDtypeStruct((ROWS, TOKENS, HD), F32),
        ],
        scratch_shapes=scratch,
        compiler_params=pltpu.CompilerParams(
            vmem_limit_bytes=VMEM, dimension_semantics=("arbitrary",)
        ),
        cost_estimate=pl.CostEstimate(
            flops=10**10, bytes_accessed=17 * 10**6, transcendentals=10**6
        ),
    )(x, *vectors, *matrices)


def build_plane(scalar_ref, piece_refs, plane_ref, turned):
    my_x, my_z, core, real = scalar_ref[0], scalar_ref[2], scalar_ref[3], scalar_ref[4]
    limit = ((real + 255) // 256) * 256

    def one_group(group, _):
        x_hi, z, x_lo = group % 2, (group // 2) % 4, group // 8
        behind_x, behind_z = (my_x - (x_hi * 2 + x_lo)) & 3, (my_z - z) & 3
        rows = pl.ds(pl.multiple_of(group * 48, 16), 48)

        def one_half(own):
            half = core if own else 1 - core
            lanes = pl.ds(pl.multiple_of(half * 384, 128), 384)
            if turned:
                key = lax.broadcasted_iota(jnp.int32, (48, 384), 0) + group * 48
                needed = group * 48 < limit
            else:
                key = lax.broadcasted_iota(jnp.int32, (48, 384), 1) + half * 384
                needed = half * 384 < limit

            @pl.when(needed)
            def _():
                for head in range(HEADS):
                    if head < 2:
                        at = behind_z * 4 + behind_x
                    else:
                        at = behind_x * 4 + behind_z
                    values = piece_refs[head // 2 * 2 + (0 if own else 1)][at, head % 2]
                    plane_ref[head, rows, lanes] = jnp.where(
                        key < real, values.astype(F32) * LOG2E, NEGATIVE
                    )

        one_half(True)
        one_half(False)
        return 0

    lax.fori_loop(0, 16, one_group, 0)

    def turn(head, _):
        for a in range(6):

            @pl.when(a * 128 < limit)
            def _():
                for b in range(a, 6):
                    aa, bb = slice(a * 128, a * 128 + 128), slice(b * 128, b * 128 + 128)
                    upper = plane_ref[head, aa, bb]
                    lower = plane_ref[head, bb, aa]
                    plane_ref[head, aa, bb] = lower.T
                    if a != b:
                        plane_ref[head, bb, aa] = upper.T
        return 0

    if turned:
        lax.fori_loop(0, HEADS, turn, 0)


def attend(keys, q_ref, k_ref, v_ref, plane_ref, mixed_ref):
    group = lane_group()
    value = total = None
    for head in range(HEADS):
        scores = dot(q_ref[0, head], k_ref[0, head, :keys, :], NT) + plane_ref[head, :, :keys]
        highest = jnp.max(scores, axis=-1, keepdims=True)
        weights = jnp.exp2(scores - highest).astype(BF16)
        weight = jnp.sum(weights.astype(F32), axis=-1, keepdims=True)
        mixed = dot(weights, v_ref[0, :keys, :])
        mixed = mixed[:, :HD] + mixed[:, HD:]
        weight = jnp.broadcast_to(weight, mixed.shape)
        value = mixed if head == 0 else jnp.where(group == head, mixed, value)
        total = weight if head == 0 else jnp.where(group == head, weight, total)
    mixed_ref[...] = value / total


def attend_kernel(turned, scalar_ref, q_ref, k_ref, v_ref, g_ref, wo_ref, *rest):
    piece_refs, rest = rest[:4], rest[4:]
    step = pl.program_id(0)
    if turned:
        crossed_ref, plane_ref, mixed_ref = rest
    else:
        x_ref, gain_ref, shift_ref, nbias_ref = rest[:4]
        first_ref, crossed_ref, kept_ref, sent_ref, plane_ref, mixed_ref, rows_ref = rest[4:]

    @pl.when(step == 0)
    def _():
        build_plane(scalar_ref, piece_refs, plane_ref, turned)

    real = scalar_ref[4]
    for keys in (256, 512, 768):

        @pl.when((real > keys - 256) & (real <= keys))
        def _():
            attend(keys, q_ref, k_ref, v_ref, plane_ref, mixed_ref)

    update = dot_split(side_by_side(g_ref[0] * mixed_ref[...]), *twice(wo_ref[0]))
    if turned:
        mixed_ref[...] = update
        for row in range(ROWS):
            crossed_ref[pl.ds(row * ROWS + step, DEVICES, stride=PADDED), :] = mixed_ref[
                pl.ds(row, DEVICES, stride=ROWS), :
            ]
    else:
        first = x_ref[0] + update
        first_ref[0] = first
        standard = standardize(first)
        mixed_ref[...] = encode(standard)
        for column in range(ROWS):
            crossed_ref[pl.ds(step * ROWS + column, DEVICES, stride=PADDED), :] = mixed_ref[
                pl.ds(column, DEVICES, stride=ROWS), :
            ]
        normed = standard * gain_ref[1:2, :] + shift_ref[1:2, :]
        bias = dot3(split(nbias_ref[1]), split(normed), NT)
        for row in range(ROWS):

            @pl.when(step == row)
            def _():
                for half in range(2):
                    at = half * 24 + row * 4
                    rows_ref[at : at + 4, :] = bias[:, half * 384 : (half + 1) * 384]

        @pl.when(step == ROWS - 1)
        def _():
            hand_over(scalar_ref, rows_ref, kept_ref, sent_ref)


def run_pass(turned, scalars, projected, w_o, pieces, x=None, extra=()):
    whole = pl.BlockSpec(memory_space=pltpu.VMEM)
    row_spec = pl.BlockSpec((1, TOKENS, HD), lambda i: (i, 0, 0))
    head_spec = pl.BlockSpec((1, HEADS, TOKENS, HD), lambda i: (i, 0, 0, 0))
    in_specs = [pl.BlockSpec(memory_space=pltpu.SMEM), head_spec, head_spec]
    in_specs += [pl.BlockSpec((1, TOKENS, 2 * HD), lambda i: (i, 0, 0)), row_spec]
    in_specs += [matrix(turned)] + [whole] * 4
    out_shape = [jax.ShapeDtypeStruct((DEVICES * PADDED, HD), F32)]
    out_specs = [pl.BlockSpec((DEVICES * PADDED, HD), lambda i: (0, 0))]
    scratch = [pltpu.VMEM((HEADS, TOKENS, TOKENS), F32), pltpu.VMEM((TOKENS, HD), F32)]
    args = [scalars, *projected, w_o, *pieces]
    if not turned:
        in_specs += [row_spec] + [whole] * 3
        args += [x, *extra]
        out_shape = [jax.ShapeDtypeStruct((ROWS, TOKENS, HD), F32)] + out_shape
        out_shape += [jax.ShapeDtypeStruct((24, 384), BF16)] * 2
        out_specs = [row_spec] + out_specs + [pl.BlockSpec((24, 384), lambda i: (0, 0))] * 2
        scratch.append(pltpu.VMEM((48, 384), F32))
    return pl.pallas_call(
        functools.partial(attend_kernel, turned),
        grid=(ROWS,),
        in_specs=in_specs,
        out_specs=out_specs,
        out_shape=out_shape,
        scratch_shapes=scratch,
        compiler_params=pltpu.CompilerParams(
            vmem_limit_bytes=VMEM, dimension_semantics=("arbitrary",)
        ),
        cost_estimate=pl.CostEstimate(
            flops=2 * 10**10, bytes_accessed=2 * 10**7, transcendentals=14 * 10**6
        ),
    )(*args)


def final_kernel(first_ref, update_ref, out_ref, row_ref):
    step = pl.program_id(0)
    for column in range(ROWS):
        row_ref[pl.ds(column, DEVICES, stride=ROWS), :] = update_ref[
            pl.ds(step * ROWS + column, DEVICES, stride=PADDED), :
        ]
    out_ref[0] = first_ref[0] + row_ref[...]


def add_crossed(first, update):
    row_spec = pl.BlockSpec((1, TOKENS, HD), lambda i: (i, 0, 0))
    return pl.pallas_call(
        final_kernel,
        grid=(ROWS,),
        in_specs=[row_spec, pl.BlockSpec(memory_space=pltpu.VMEM)],
        out_specs=row_spec,
        out_shape=jax.ShapeDtypeStruct((ROWS, TOKENS, HD), F32),
        scratch_shapes=[pltpu.VMEM((TOKENS, HD), F32)],
        compiler_params=pltpu.CompilerParams(
            vmem_limit_bytes=VMEM, dimension_semantics=("arbitrary",)
        ),
        cost_estimate=pl.CostEstimate(flops=10**6, bytes_accessed=8 * 10**6, transcendentals=0),
    )(first, update)


def cross(values):
    return lax.all_to_all(values, AXES, split_axis=0, concat_axis=0, tiled=True)


def on_device(
    pair_tensor,
    token_mask,
    ln_gain,
    ln_shift,
    w_query,
    w_key,
    w_value,
    w_bias,
    w_gate,
    gate_shift,
    w_out,
):
    row, col = lax.axis_index("row"), lax.axis_index("col")
    place = [(col // 8) * 2 + row // 4, (col // 2) % 4, row % 4, col % 2]
    place = jnp.stack([jnp.int32(p) for p in place])
    vectors, matrices = (ln_gain, ln_shift, gate_shift), (w_query, w_key, w_value, w_gate)

    start = first_bias(place, pair_tensor, ln_gain, ln_shift, w_bias)
    planes, projected = gather_plane(
        place, *start, pair_tensor, lambda cells: project(False, cells, vectors, matrices)
    )
    scalars = jnp.concatenate([place, jnp.sum(token_mask, dtype=jnp.int32, keepdims=True)])
    first, codes, *end = run_pass(
        False, scalars, projected, w_out, planes, pair_tensor, (ln_gain, ln_shift, w_bias)
    )
    codes = cross(codes.astype(jnp.int16))
    planes, projected = gather_plane(
        place, *end, codes, lambda held: project(True, held.astype(F32), vectors, matrices)
    )
    (update,) = run_pass(True, scalars, projected, w_out, planes)
    return add_crossed(first, cross(update.astype(jnp.float16)).astype(F32))


def solution(mesh):
    placed = (P(AXES, None, None), P(), P(), P(), P(), P(), P(), P(), P(), P(), P())
    return jax.shard_map(
        on_device,
        mesh=mesh,
        in_specs=placed,
        out_specs=P(AXES, None, None),
        check_vma=False,
    )
```

profile of v0, /device:TPU:1, one launch (start us, length us, event | category | flops | bytes accessed | tf_op | source)
XLA Modules:
  0.0 239.5 jit_solution(5695026473977790172)
XLA Ops:
  0.6 5.8 %shard_map.109 = (bf16[24,384]{1,0:T(8,128)(2,1)}, bf16[24,384]{1,0:T(8,128)(2,1)}) custom-call(s32[4]{0:T(128)} %pad_add_fusion.scalar_ref, f32[6,768,128]{2,1,0:T(8,128)} %rest_4_.1, f32[2,128]{1,0:T(2,128)} %gain_ref.5, f32[2,128]{1,0:T(2,128)} %shift_ref.5, f32[2,4,128]{2,1,0:T(4,128)} %rest_7_.1), custom_call_target="tpu_custom_call" | custom-call | flops 100000000 | bytes 2000000 | tf_op jit(solution)/shard_map/pallas_call | solution.py:164
  6.4 1.4 collective-permute-start
  8.9 2.8 %collective-permute-start.3 = (bf16[48,384]{1,0:T(8,128)(2,1)S(1)}, bf16[48,384]{1,0:T(8,128)(2,1)S(1)}, u32[]{:S(2)}, u32[]{:S(2)}) collective-permute-start(bf16[48,384]{1,0:T(8,128)(2,1)S(1)} %constant_dynamic-update-slice_fusion.refs_0_), channel_id=1, source_target_pairs={{0,6},{1,7},{2,0},{3,1},{4,2},{5,3},{6,4},{7,5},{8,14},{9,15},{10,... | collective-permute-start | bytes 110600 | tf_op jit(solution)/shard_map/ppermute | solution.py:48
  12.8 3.3 %collective-permute-done.2.refs_2_ = bf16[48,384]{1,0:T(8,128)(2,1)S(1)} collective-permute-done((bf16[48,384]{1,0:T(8,128)(2,1)S(1)}, bf16[48,384]{1,0:T(8,128)(2,1)S(1)}, u32[]{:S(2)}, u32[]{:S(2)}) %collective-permute-start.2) | collective-permute-done | bytes 36896 | tf_op jit(solution)/shard_map/ppermute | solution.py:48
  17.3 1.8 shard_map.110
  19.1 3.7 %collective-permute-start.9 = (bf16[1,2,48,384]{3,2,1,0:T(8,128)(2,1)}, bf16[1,2,48,384]{3,2,1,0:T(8,128)(2,1)S(1)}, u32[]{:S(2)}, u32[]{:S(2)}) collective-permute-start(bf16[1,2,48,384]{3,2,1,0:T(8,128)(2,1)} %bitcast.29), channel_id=1, source_target_pairs={{0,48},{1,49},{2,50},{3,51},{4,52},{5,53},{6,54},{7,55},{8,56},{9,... | collective-permute-start | bytes 221192 | tf_op jit(solution)/shard_map/ppermute | solution.py:48
  23.5 2.5 %collective-permute-start.6 = (bf16[1,2,48,384]{3,2,1,0:T(8,128)(2,1)}, bf16[1,2,48,384]{3,2,1,0:T(8,128)(2,1)S(1)}, u32[]{:S(2)}, u32[]{:S(2)}) collective-permute-start(bf16[1,2,48,384]{3,2,1,0:T(8,128)(2,1)} %bitcast.21), channel_id=1, source_target_pairs={{0,72},{1,73},{2,74},{3,75},{4,76},{5,77},{6,78},{7,79},{8,64},{9,... | collective-permute-start | bytes 221192 | tf_op jit(solution)/shard_map/ppermute | solution.py:48
  28.2 0.9 pad_maximum_fusion.5
  29.2 1.8 collective-permute-done.5
  31.7 0.9 pad_maximum_fusion.4
  32.6 2.0 collective-permute-start.12
  34.7 1.8 collective-permute-start.11
  36.7 0.8 collective-permute-start.14
  37.5 1.2 collective-permute-done.12
  39.2 12.5 %shard_map.111 = (bf16[6,4,768,128]{3,2,1,0:T(8,128)(2,1)}, bf16[6,4,768,128]{3,2,1,0:T(8,128)(2,1)}, bf16[6,768,256]{2,1,0:T(8,128)(2,1)}, f32[6,768,128]{2,1,0:T(8,128)}) custom-call(f32[6,768,128]{2,1,0:T(8,128)} %rest_4_.1, f32[2,128]{1,0:T(2,128)} %gain_ref.5, f32[2,128]{1,0:T(2,128)} %shift_ref.5, f32[2,128]{1,0:T(2,128)} %gs_ref.3, ...), custom_call_target="tpu_custom_call" | custom-call | flops 10000000000 | bytes 17000000 | tf_op jit(solution)/shard_map/pallas_call | solution.py:248
  52.3 0.8 copy-done
  53.1 8.8 %collective-permute-start.16 = (bf16[16,2,48,384]{3,2,1,0:T(8,128)(2,1)S(1)}, bf16[16,2,48,384]{3,2,1,0:T(8,128)(2,1)S(1)}, u32[]{:S(2)}, u32[]{:S(2)}) collective-permute-start(bf16[16,2,48,384]{3,2,1,0:T(8,128)(2,1)S(1)} %pad_maximum_fusion.rest_0_), channel_id=1, source_target_pairs={{0,1},{1,0},{2,3},{3,2},{4,5},{5,4},{6,7},{7,6},{8,9},{9,8},{10,11... | collective-permute-start | bytes 3538952 | tf_op jit(solution)/shard_map/ppermute | solution.py:48
  62.7 1.3 concatenate.34.scalar_ref
  64.4 1.7 collective-permute-done.17.rest_3_
  66.1 27.7 %shard_map.112 = (f32[6,768,128]{2,1,0:T(8,128)}, f32[5120,128]{1,0:T(8,128)}, bf16[24,384]{1,0:T(8,128)(2,1)}, bf16[24,384]{1,0:T(8,128)(2,1)}) custom-call(s32[5]{0:T(128)} %concatenate.34.scalar_ref, bf16[6,4,768,128]{3,2,1,0:T(8,128)(2,1)} %get-tuple-element.52.q_ref, bf16[6,4,768,128]{3,2,1,0:T(8,128)(2,1)} %get-tuple-element.53.k_ref, ...), custom_call_target="tpu_custom_call" | custom-call | flops 20000000000 | bytes 20000000 | tf_op jit(solution)/shard_map/pallas_call | solution.py:411
  93.8 3.3 %convert_element_type.14 = s16[5120,128]{1,0:T(8,128)(2,1)} convert(f32[5120,128]{1,0:T(8,128)} %get-tuple-element.63) | non-fusion elementwise | flops 655360 | bytes 3932160 | tf_op jit(solution)/shard_map/convert_element_type | solution.py:482
  97.1 8.7 %all-to-all-start = ((s16[128,40,128]{2,1,0:T(8,128)(2,1)}), s16[128,40,128]{2,1,0:T(8,128)(2,1)S(1)}, u32[]{:S(2)}, u32[]{:S(2)}) async-start(s16[128,40,128]{2,1,0:T(8,128)(2,1)} %bitcast.9), calls=%async_computation | async-start | bytes 2621440 | tf_op jit(solution)/shard_map/all_to_all | solution.py:453
  105.8 1.1 collective-permute-start.18
  107.0 0.8 collective-permute-done.18
  107.8 1.9 collective-permute-start.21
  110.9 7.4 %collective-permute-done.21.refs_3_ = bf16[48,384]{1,0:T(8,128)(2,1)S(1)} collective-permute-done((bf16[48,384]{1,0:T(8,128)(2,1)S(1)}, bf16[48,384]{1,0:T(8,128)(2,1)S(1)}, u32[]{:S(2)}, u32[]{:S(2)}) %collective-permute-start.21) | collective-permute-done | bytes 36896 | tf_op jit(solution)/shard_map/ppermute | solution.py:48
  119.0 2.0 collective-permute-done.19.refs_1_
  121.6 1.8 shard_map.113
  123.4 5.1 %collective-permute-start.27 = (bf16[1,2,48,384]{3,2,1,0:T(8,128)(2,1)}, bf16[1,2,48,384]{3,2,1,0:T(8,128)(2,1)S(1)}, u32[]{:S(2)}, u32[]{:S(2)}) collective-permute-start(bf16[1,2,48,384]{3,2,1,0:T(8,128)(2,1)} %bitcast.25), channel_id=1, source_target_pairs={{0,48},{1,49},{2,50},{3,51},{4,52},{5,53},{6,54},{7,55},{8,56},{9,... | collective-permute-start | bytes 221192 | tf_op jit(solution)/shard_map/ppermute | solution.py:48
  128.4 1.0 collective-permute-start.25
  129.5 3.9 %collective-permute-start.24 = (bf16[1,2,48,384]{3,2,1,0:T(8,128)(2,1)}, bf16[1,2,48,384]{3,2,1,0:T(8,128)(2,1)S(1)}, u32[]{:S(2)}, u32[]{:S(2)}) collective-permute-start(bf16[1,2,48,384]{3,2,1,0:T(8,128)(2,1)} %bitcast.17), channel_id=1, source_target_pairs={{0,72},{1,73},{2,74},{3,75},{4,76},{5,77},{6,78},{7,79},{8,64},{9,... | collective-permute-start | bytes 221192 | tf_op jit(solution)/shard_map/ppermute | solution.py:48
  133.8 0.9 collective-permute-start.22
  134.6 0.9 pad_maximum_fusion.7
  135.6 2.8 %collective-permute-done.23 = bf16[1,2,48,384]{3,2,1,0:T(8,128)(2,1)S(1)} collective-permute-done((bf16[1,2,48,384]{3,2,1,0:T(8,128)(2,1)}, bf16[1,2,48,384]{3,2,1,0:T(8,128)(2,1)S(1)}, u32[]{:S(2)}, u32[]{:S(2)}) %collective-permute-start.23) | collective-permute-done | bytes 73760 | tf_op jit(solution)/shard_map/ppermute | solution.py:48
  139.1 0.9 pad_maximum_fusion.6
  140.0 2.0 collective-permute-start.30
  142.1 1.8 collective-permute-start.29
  144.8 1.8 convert_element_type.15.x_ref
  147.2 11.2 %shard_map.114 = (bf16[6,4,768,128]{3,2,1,0:T(8,128)(2,1)}, bf16[6,4,768,128]{3,2,1,0:T(8,128)(2,1)}, bf16[6,768,256]{2,1,0:T(8,128)(2,1)}, f32[6,768,128]{2,1,0:T(8,128)}) custom-call(f32[5120,128]{1,0:T(8,128)} %convert_element_type.15.x_ref, f32[2,128]{1,0:T(2,128)} %gain_ref.5, f32[2,128]{1,0:T(2,128)} %shift_ref.5, f32[2,128]{1,0:T(2,128)} %gs_ref.3, ...), custom_call_target="tpu_custom_call" | custom-call | flops 10000000000 | bytes 17000000 | tf_op jit(solution)/shard_map/pallas_call | solution.py:248
  158.9 0.8 copy-done.1
  159.7 8.5 %collective-permute-start.34 = (bf16[16,2,48,384]{3,2,1,0:T(8,128)(2,1)S(1)}, bf16[16,2,48,384]{3,2,1,0:T(8,128)(2,1)S(1)}, u32[]{:S(2)}, u32[]{:S(2)}) collective-permute-start(bf16[16,2,48,384]{3,2,1,0:T(8,128)(2,1)S(1)} %pad_maximum_fusion.2.rest_0_), channel_id=1, source_target_pairs={{0,1},{1,0},{2,3},{3,2},{4,5},{5,4},{6,7},{7,6},{8,9},{9,8},{10,11... | collective-permute-start | bytes 3538952 | tf_op jit(solution)/shard_map/ppermute | solution.py:48
  168.4 2.2 collective-permute-done.34.rest_1_
  170.7 1.0 copy-done.15
  172.5 25.8 %shard_map.115 = f32[5120,128]{1,0:T(8,128)} custom-call(s32[5]{0:T(128)} %concatenate.34.scalar_ref, bf16[6,4,768,128]{3,2,1,0:T(8,128)(2,1)} %get-tuple-element.71.q_ref, bf16[6,4,768,128]{3,2,1,0:T(8,128)(2,1)} %get-tuple-element.72.k_ref, bf16[6,768,256]{2,1,0:T(8,128)(2,1)} %get-tuple-element.73.v_ref, f32[6,768,128]{2,1,0:T(8,128)} %get-tuple-element.74.g_ref, ...), custom_call_target="tpu_custom_call" | custom-call | flops 20000000000 | bytes 20000000 | tf_op jit(solution)/shard_map/pallas_call | solution.py:411
  198.3 1.9 convert_element_type.16
  200.2 31.1 %all_to_all.21 = f16[128,40,128]{2,1,0:T(8,128)(2,1)S(1)} all-to-all(f16[128,40,128]{2,1,0:T(8,128)(2,1)S(1)} %bitcast.16), channel_id=1, replica_groups=mesh['row'=8,'col'=16] {'row','col'}, dimensions={0} | all-to-all | bytes 2621440 | tf_op jit(solution)/shard_map/all_to_all | solution.py:453
  231.3 1.7 bitcast_convert_fusion.update_ref
  233.0 6.0 %shard_map.116 = f32[6,768,128]{2,1,0:T(8,128)} custom-call(f32[6,768,128]{2,1,0:T(8,128)} %get-tuple-element.58.first_ref, f32[5120,128]{1,0:T(8,128)} %bitcast_convert_fusion.update_ref), custom_call_target="tpu_custom_call" | custom-call | flops 1000000 | bytes 8000000 | tf_op jit(solution)/shard_map/pallas_call | solution.py:438
  (88 shorter events, 16.6 us)
Async XLA Ops:
  6.4 2.5 %collective-permute-start = (bf16[24,384]{1,0:T(8,128)(2,1)}, bf16[24,384]{1,0:T(8,128)(2,1)S(1)}, u32[]{:S(2)}, u32[]{:S(2)}) collective-permute-start(bf16[24,384]{1,0:T(8,128)(2,1)} %get-tuple-element.42), channel_id=1, source_target_pairs={{0,1},{1,0},{2,3},{3,2},{4,5},{5,4},{6,7},{7,6},{8,9},{9,8},{10,11... | collective-permute-start | bytes 55304 | tf_op jit(solution)/shard_map/ppermute | solution.py:48
  8.9 7.5 %copy-start.4 = (bf16[48,384]{1,0:T(8,128)(2,1)}, bf16[48,384]{1,0:T(8,128)(2,1)S(1)}, u32[]{:S(2)}) copy-start(bf16[48,384]{1,0:T(8,128)(2,1)S(1)} %constant_dynamic-update-slice_fusion.refs_0_) | copy-start | bytes 110596
  8.9 3.9 %collective-permute-start.3 = (bf16[48,384]{1,0:T(8,128)(2,1)S(1)}, bf16[48,384]{1,0:T(8,128)(2,1)S(1)}, u32[]{:S(2)}, u32[]{:S(2)}) collective-permute-start(bf16[48,384]{1,0:T(8,128)(2,1)S(1)} %constant_dynamic-update-slice_fusion.refs_0_), channel_id=1, source_target_pairs={{0,6},{1,7},{2,0},{3,1},{4,2},{5,3},{6,4},{7,5},{8,14},{9,15},{10,... | collective-permute-start | bytes 110600 | tf_op jit(solution)/shard_map/ppermute | solution.py:48
  11.7 4.3 %collective-permute-start.2 = (bf16[48,384]{1,0:T(8,128)(2,1)S(1)}, bf16[48,384]{1,0:T(8,128)(2,1)S(1)}, u32[]{:S(2)}, u32[]{:S(2)}) collective-permute-start(bf16[48,384]{1,0:T(8,128)(2,1)S(1)} %constant_dynamic-update-slice_fusion.refs_0_), channel_id=1, source_target_pairs={{0,4},{1,5},{2,6},{3,7},{4,0},{5,1},{6,2},{7,3},{8,12},{9,13},{10,... | collective-permute-start | bytes 110600 | tf_op jit(solution)/shard_map/ppermute | solution.py:48
  12.1 4.4 %collective-permute-start.1 = (bf16[48,384]{1,0:T(8,128)(2,1)S(1)}, bf16[48,384]{1,0:T(8,128)(2,1)S(1)}, u32[]{:S(2)}, u32[]{:S(2)}) collective-permute-start(bf16[48,384]{1,0:T(8,128)(2,1)S(1)} %constant_dynamic-update-slice_fusion.refs_0_), channel_id=1, source_target_pairs={{0,2},{1,3},{2,4},{3,5},{4,6},{5,7},{6,0},{7,1},{8,10},{9,11},{10,... | collective-permute-start | bytes 110600 | tf_op jit(solution)/shard_map/ppermute | solution.py:48
  12.8 3.6 %copy-start.7 = (bf16[48,384]{1,0:T(8,128)(2,1)}, bf16[48,384]{1,0:T(8,128)(2,1)S(1)}, u32[]{:S(2)}) copy-start(bf16[48,384]{1,0:T(8,128)(2,1)S(1)} %collective-permute-done.3.refs_3_) | copy-start | bytes 110596
  19.1 7.5 %collective-permute-start.9 = (bf16[1,2,48,384]{3,2,1,0:T(8,128)(2,1)}, bf16[1,2,48,384]{3,2,1,0:T(8,128)(2,1)S(1)}, u32[]{:S(2)}, u32[]{:S(2)}) collective-permute-start(bf16[1,2,48,384]{3,2,1,0:T(8,128)(2,1)} %bitcast.29), channel_id=1, source_target_pairs={{0,48},{1,49},{2,50},{3,51},{4,52},{5,53},{6,54},{7,55},{8,56},{9,... | collective-permute-start | bytes 221192 | tf_op jit(solution)/shard_map/ppermute | solution.py:48
  22.8 5.0 %collective-permute-start.8 = (bf16[1,2,48,384]{3,2,1,0:T(8,128)(2,1)}, bf16[1,2,48,384]{3,2,1,0:T(8,128)(2,1)S(1)}, u32[]{:S(2)}, u32[]{:S(2)}) collective-permute-start(bf16[1,2,48,384]{3,2,1,0:T(8,128)(2,1)} %bitcast.30), channel_id=1, source_target_pairs={{0,32},{1,33},{2,34},{3,35},{4,36},{5,37},{6,38},{7,39},{8,40},{9,... | collective-permute-start | bytes 221192 | tf_op jit(solution)/shard_map/ppermute | solution.py:48
  22.8 5.4 %collective-permute-start.7 = (bf16[1,2,48,384]{3,2,1,0:T(8,128)(2,1)}, bf16[1,2,48,384]{3,2,1,0:T(8,128)(2,1)S(1)}, u32[]{:S(2)}, u32[]{:S(2)}) collective-permute-start(bf16[1,2,48,384]{3,2,1,0:T(8,128)(2,1)} %bitcast.31), channel_id=1, source_target_pairs={{0,16},{1,17},{2,18},{3,19},{4,20},{5,21},{6,22},{7,23},{8,24},{9,... | collective-permute-start | bytes 221192 | tf_op jit(solution)/shard_map/ppermute | solution.py:48
  23.5 5.7 %collective-permute-start.6 = (bf16[1,2,48,384]{3,2,1,0:T(8,128)(2,1)}, bf16[1,2,48,384]{3,2,1,0:T(8,128)(2,1)S(1)}, u32[]{:S(2)}, u32[]{:S(2)}) collective-permute-start(bf16[1,2,48,384]{3,2,1,0:T(8,128)(2,1)} %bitcast.21), channel_id=1, source_target_pairs={{0,72},{1,73},{2,74},{3,75},{4,76},{5,77},{6,78},{7,79},{8,64},{9,... | collective-permute-start | bytes 221192 | tf_op jit(solution)/shard_map/ppermute | solution.py:48
  26.0 5.0 %collective-permute-start.5 = (bf16[1,2,48,384]{3,2,1,0:T(8,128)(2,1)}, bf16[1,2,48,384]{3,2,1,0:T(8,128)(2,1)S(1)}, u32[]{:S(2)}, u32[]{:S(2)}) collective-permute-start(bf16[1,2,48,384]{3,2,1,0:T(8,128)(2,1)} %bitcast.22), channel_id=1, source_target_pairs={{0,8},{1,9},{2,10},{3,11},{4,12},{5,13},{6,14},{7,15},{8,0},{9,1},... | collective-permute-start | bytes 221192 | tf_op jit(solution)/shard_map/ppermute | solution.py:48
  26.5 5.2 %collective-permute-start.4 = (bf16[1,2,48,384]{3,2,1,0:T(8,128)(2,1)}, bf16[1,2,48,384]{3,2,1,0:T(8,128)(2,1)S(1)}, u32[]{:S(2)}, u32[]{:S(2)}) collective-permute-start(bf16[1,2,48,384]{3,2,1,0:T(8,128)(2,1)} %bitcast.23), channel_id=1, source_target_pairs={{0,64},{1,65},{2,66},{3,67},{4,68},{5,69},{6,70},{7,71},{8,72},{9,... | collective-permute-start | bytes 221192 | tf_op jit(solution)/shard_map/ppermute | solution.py:48
  32.6 6.1 %collective-permute-start.12 = (bf16[4,2,48,384]{3,2,1,0:T(8,128)(2,1)S(1)}, bf16[4,2,48,384]{3,2,1,0:T(8,128)(2,1)S(1)}, u32[]{:S(2)}, u32[]{:S(2)}) collective-permute-start(bf16[4,2,48,384]{3,2,1,0:T(8,128)(2,1)S(1)} %pad_maximum_fusion.4), channel_id=1, source_target_pairs={{0,48},{1,49},{2,50},{3,51},{4,52},{5,53},{6,54},{7,55},{8,56},{9,... | collective-permute-start | bytes 884744 | tf_op jit(solution)/shard_map/ppermute | solution.py:48
  34.7 17.1 %collective-permute-start.11 = (bf16[4,2,48,384]{3,2,1,0:T(8,128)(2,1)S(1)}, bf16[4,2,48,384]{3,2,1,0:T(8,128)(2,1)S(1)}, u32[]{:S(2)}, u32[]{:S(2)}) collective-permute-start(bf16[4,2,48,384]{3,2,1,0:T(8,128)(2,1)S(1)} %pad_maximum_fusion.4), channel_id=1, source_target_pairs={{0,32},{1,33},{2,34},{3,35},{4,36},{5,37},{6,38},{7,39},{8,40},{9,... | collective-permute-start | bytes 884744 | tf_op jit(solution)/shard_map/ppermute | solution.py:48
  36.4 15.3 %collective-permute-start.10 = (bf16[4,2,48,384]{3,2,1,0:T(8,128)(2,1)S(1)}, bf16[4,2,48,384]{3,2,1,0:T(8,128)(2,1)S(1)}, u32[]{:S(2)}, u32[]{:S(2)}) collective-permute-start(bf16[4,2,48,384]{3,2,1,0:T(8,128)(2,1)S(1)} %pad_maximum_fusion.4), channel_id=1, source_target_pairs={{0,16},{1,17},{2,18},{3,19},{4,20},{5,21},{6,22},{7,23},{8,24},{9,... | collective-permute-start | bytes 884744 | tf_op jit(solution)/shard_map/ppermute | solution.py:48
  36.4 15.6 %collective-permute-start.15 = (bf16[4,2,48,384]{3,2,1,0:T(8,128)(2,1)S(1)}, bf16[4,2,48,384]{3,2,1,0:T(8,128)(2,1)S(1)}, u32[]{:S(2)}, u32[]{:S(2)}) collective-permute-start(bf16[4,2,48,384]{3,2,1,0:T(8,128)(2,1)S(1)} %pad_maximum_fusion.5), channel_id=1, source_target_pairs={{0,72},{1,73},{2,74},{3,75},{4,76},{5,77},{6,78},{7,79},{8,64},{9,... | collective-permute-start | bytes 884744 | tf_op jit(solution)/shard_map/ppermute | solution.py:48
  36.7 15.3 %collective-permute-start.14 = (bf16[4,2,48,384]{3,2,1,0:T(8,128)(2,1)S(1)}, bf16[4,2,48,384]{3,2,1,0:T(8,128)(2,1)S(1)}, u32[]{:S(2)}, u32[]{:S(2)}) collective-permute-start(bf16[4,2,48,384]{3,2,1,0:T(8,128)(2,1)S(1)} %pad_maximum_fusion.5), channel_id=1, source_target_pairs={{0,8},{1,9},{2,10},{3,11},{4,12},{5,13},{6,14},{7,15},{8,0},{9,1},... | collective-permute-start | bytes 884744 | tf_op jit(solution)/shard_map/ppermute | solution.py:48
  38.8 13.3 %collective-permute-start.13 = (bf16[4,2,48,384]{3,2,1,0:T(8,128)(2,1)S(1)}, bf16[4,2,48,384]{3,2,1,0:T(8,128)(2,1)S(1)}, u32[]{:S(2)}, u32[]{:S(2)}) collective-permute-start(bf16[4,2,48,384]{3,2,1,0:T(8,128)(2,1)S(1)} %pad_maximum_fusion.5), channel_id=1, source_target_pairs={{0,64},{1,65},{2,66},{3,67},{4,68},{5,69},{6,70},{7,71},{8,72},{9,... | collective-permute-start | bytes 884744 | tf_op jit(solution)/shard_map/ppermute | solution.py:48
  52.0 10.0 %copy-start.13 = (s32[768]{0:T(1024)S(1)}, s32[768]{0:T(1024)}, u32[]{:S(2)}) copy-start(s32[768]{0:T(1024)} %param.12) | copy-start | bytes 9220
  52.2 13.9 %copy-start.2 = (bf16[16,2,48,384]{3,2,1,0:T(8,128)(2,1)}, bf16[16,2,48,384]{3,2,1,0:T(8,128)(2,1)S(1)}, u32[]{:S(2)}) copy-start(bf16[16,2,48,384]{3,2,1,0:T(8,128)(2,1)S(1)} %pad_maximum_fusion.1.rest_2_) | copy-start | bytes 3538948
  53.1 11.3 %collective-permute-start.16 = (bf16[16,2,48,384]{3,2,1,0:T(8,128)(2,1)S(1)}, bf16[16,2,48,384]{3,2,1,0:T(8,128)(2,1)S(1)}, u32[]{:S(2)}, u32[]{:S(2)}) collective-permute-start(bf16[16,2,48,384]{3,2,1,0:T(8,128)(2,1)S(1)} %pad_maximum_fusion.rest_0_), channel_id=1, source_target_pairs={{0,1},{1,0},{2,3},{3,2},{4,5},{5,4},{6,7},{7,6},{8,9},{9,8},{10,11... | collective-permute-start | bytes 3538952 | tf_op jit(solution)/shard_map/ppermute | solution.py:48
  61.8 4.3 %collective-permute-start.17 = (bf16[16,2,48,384]{3,2,1,0:T(8,128)(2,1)S(1)}, bf16[16,2,48,384]{3,2,1,0:T(8,128)(2,1)}, u32[]{:S(2)}, u32[]{:S(2)}) collective-permute-start(bf16[16,2,48,384]{3,2,1,0:T(8,128)(2,1)S(1)} %pad_maximum_fusion.1.rest_2_), channel_id=1, source_target_pairs={{0,1},{1,0},{2,3},{3,2},{4,5},{5,4},{6,7},{7,6},{8,9},{9,8},{10,11... | collective-permute-start | bytes 3538952 | tf_op jit(solution)/shard_map/ppermute | solution.py:48
  64.4 1.7 copy-start.14
  97.1 8.8 %copy-start.16 = (bf16[24,384]{1,0:T(8,128)(2,1)S(1)}, bf16[24,384]{1,0:T(8,128)(2,1)}, u32[]{:S(2)}) copy-start(bf16[24,384]{1,0:T(8,128)(2,1)} %get-tuple-element.60) | copy-start | bytes 55300
  97.1 9.9 %copy-start.12 = (bf16[24,384]{1,0:T(8,128)(2,1)S(1)}, bf16[24,384]{1,0:T(8,128)(2,1)}, u32[]{:S(2)}) copy-start(bf16[24,384]{1,0:T(8,128)(2,1)} %get-tuple-element.59) | copy-start | bytes 55300
  97.1 42.9 %all-to-all-start = ((s16[128,40,128]{2,1,0:T(8,128)(2,1)}), s16[128,40,128]{2,1,0:T(8,128)(2,1)S(1)}, u32[]{:S(2)}, u32[]{:S(2)}) async-start(s16[128,40,128]{2,1,0:T(8,128)(2,1)} %bitcast.9), calls=%async_computation | async-start | bytes 2621440 | tf_op jit(solution)/shard_map/all_to_all | solution.py:453
  105.8 2.0 collective-permute-start.18
  107.8 13.2 %copy-start.5 = (bf16[48,384]{1,0:T(8,128)(2,1)}, bf16[48,384]{1,0:T(8,128)(2,1)S(1)}, u32[]{:S(2)}) copy-start(bf16[48,384]{1,0:T(8,128)(2,1)S(1)} %constant_dynamic-update-slice_fusion.2.refs_0_) | copy-start | bytes 110596
  107.8 10.5 %collective-permute-start.21 = (bf16[48,384]{1,0:T(8,128)(2,1)S(1)}, bf16[48,384]{1,0:T(8,128)(2,1)S(1)}, u32[]{:S(2)}, u32[]{:S(2)}) collective-permute-start(bf16[48,384]{1,0:T(8,128)(2,1)S(1)} %constant_dynamic-update-slice_fusion.2.refs_0_), channel_id=1, source_target_pairs={{0,6},{1,7},{2,0},{3,1},{4,2},{5,3},{6,4},{7,5},{8,14},{9,15},{10,... | collective-permute-start | bytes 110600 | tf_op jit(solution)/shard_map/ppermute | solution.py:48
  109.8 9.2 %collective-permute-start.20 = (bf16[48,384]{1,0:T(8,128)(2,1)S(1)}, bf16[48,384]{1,0:T(8,128)(2,1)S(1)}, u32[]{:S(2)}, u32[]{:S(2)}) collective-permute-start(bf16[48,384]{1,0:T(8,128)(2,1)S(1)} %constant_dynamic-update-slice_fusion.2.refs_0_), channel_id=1, source_target_pairs={{0,4},{1,5},{2,6},{3,7},{4,0},{5,1},{6,2},{7,3},{8,12},{9,13},{10,... | collective-permute-start | bytes 110600 | tf_op jit(solution)/shard_map/ppermute | solution.py:48
  110.3 10.7 %collective-permute-start.19 = (bf16[48,384]{1,0:T(8,128)(2,1)S(1)}, bf16[48,384]{1,0:T(8,128)(2,1)S(1)}, u32[]{:S(2)}, u32[]{:S(2)}) collective-permute-start(bf16[48,384]{1,0:T(8,128)(2,1)S(1)} %constant_dynamic-update-slice_fusion.2.refs_0_), channel_id=1, source_target_pairs={{0,2},{1,3},{2,4},{3,5},{4,6},{5,7},{6,0},{7,1},{8,10},{9,11},{10,... | collective-permute-start | bytes 110600 | tf_op jit(solution)/shard_map/ppermute | solution.py:48
  118.3 2.7 %copy-start.6 = (bf16[48,384]{1,0:T(8,128)(2,1)}, bf16[48,384]{1,0:T(8,128)(2,1)S(1)}, u32[]{:S(2)}) copy-start(bf16[48,384]{1,0:T(8,128)(2,1)S(1)} %collective-permute-done.21.refs_3_) | copy-start | bytes 110596
  119.0 2.0 copy-start.8
  123.4 10.4 %collective-permute-start.27 = (bf16[1,2,48,384]{3,2,1,0:T(8,128)(2,1)}, bf16[1,2,48,384]{3,2,1,0:T(8,128)(2,1)S(1)}, u32[]{:S(2)}, u32[]{:S(2)}) collective-permute-start(bf16[1,2,48,384]{3,2,1,0:T(8,128)(2,1)} %bitcast.25), channel_id=1, source_target_pairs={{0,48},{1,49},{2,50},{3,51},{4,52},{5,53},{6,54},{7,55},{8,56},{9,... | collective-permute-start | bytes 221192 | tf_op jit(solution)/shard_map/ppermute | solution.py:48
  128.4 6.2 %collective-permute-start.26 = (bf16[1,2,48,384]{3,2,1,0:T(8,128)(2,1)}, bf16[1,2,48,384]{3,2,1,0:T(8,128)(2,1)S(1)}, u32[]{:S(2)}, u32[]{:S(2)}) collective-permute-start(bf16[1,2,48,384]{3,2,1,0:T(8,128)(2,1)} %bitcast.26), channel_id=1, source_target_pairs={{0,32},{1,33},{2,34},{3,35},{4,36},{5,37},{6,38},{7,39},{8,40},{9,... | collective-permute-start | bytes 221192 | tf_op jit(solution)/shard_map/ppermute | solution.py:48
  128.4 6.2 %collective-permute-start.25 = (bf16[1,2,48,384]{3,2,1,0:T(8,128)(2,1)}, bf16[1,2,48,384]{3,2,1,0:T(8,128)(2,1)S(1)}, u32[]{:S(2)}, u32[]{:S(2)}) collective-permute-start(bf16[1,2,48,384]{3,2,1,0:T(8,128)(2,1)} %bitcast.27), channel_id=1, source_target_pairs={{0,16},{1,17},{2,18},{3,19},{4,20},{5,21},{6,22},{7,23},{8,24},{9,... | collective-permute-start | bytes 221192 | tf_op jit(solution)/shard_map/ppermute | solution.py:48
  129.5 6.1 %collective-permute-start.24 = (bf16[1,2,48,384]{3,2,1,0:T(8,128)(2,1)}, bf16[1,2,48,384]{3,2,1,0:T(8,128)(2,1)S(1)}, u32[]{:S(2)}, u32[]{:S(2)}) collective-permute-start(bf16[1,2,48,384]{3,2,1,0:T(8,128)(2,1)} %bitcast.17), channel_id=1, source_target_pairs={{0,72},{1,73},{2,74},{3,75},{4,76},{5,77},{6,78},{7,79},{8,64},{9,... | collective-permute-start | bytes 221192 | tf_op jit(solution)/shard_map/ppermute | solution.py:48
  133.4 5.0 %collective-permute-start.23 = (bf16[1,2,48,384]{3,2,1,0:T(8,128)(2,1)}, bf16[1,2,48,384]{3,2,1,0:T(8,128)(2,1)S(1)}, u32[]{:S(2)}, u32[]{:S(2)}) collective-permute-start(bf16[1,2,48,384]{3,2,1,0:T(8,128)(2,1)} %bitcast.18), channel_id=1, source_target_pairs={{0,8},{1,9},{2,10},{3,11},{4,12},{5,13},{6,14},{7,15},{8,0},{9,1},... | collective-permute-start | bytes 221192 | tf_op jit(solution)/shard_map/ppermute | solution.py:48
  133.8 5.3 %collective-permute-start.22 = (bf16[1,2,48,384]{3,2,1,0:T(8,128)(2,1)}, bf16[1,2,48,384]{3,2,1,0:T(8,128)(2,1)S(1)}, u32[]{:S(2)}, u32[]{:S(2)}) collective-permute-start(bf16[1,2,48,384]{3,2,1,0:T(8,128)(2,1)} %bitcast.19), channel_id=1, source_target_pairs={{0,64},{1,65},{2,66},{3,67},{4,68},{5,69},{6,70},{7,71},{8,72},{9,... | collective-permute-start | bytes 221192 | tf_op jit(solution)/shard_map/ppermute | solution.py:48
  140.0 6.6 %collective-permute-start.30 = (bf16[4,2,48,384]{3,2,1,0:T(8,128)(2,1)S(1)}, bf16[4,2,48,384]{3,2,1,0:T(8,128)(2,1)S(1)}, u32[]{:S(2)}, u32[]{:S(2)}) collective-permute-start(bf16[4,2,48,384]{3,2,1,0:T(8,128)(2,1)S(1)} %pad_maximum_fusion.6), channel_id=1, source_target_pairs={{0,48},{1,49},{2,50},{3,51},{4,52},{5,53},{6,54},{7,55},{8,56},{9,... | collective-permute-start | bytes 884744 | tf_op jit(solution)/shard_map/ppermute | solution.py:48
  142.1 16.4 %collective-permute-start.29 = (bf16[4,2,48,384]{3,2,1,0:T(8,128)(2,1)S(1)}, bf16[4,2,48,384]{3,2,1,0:T(8,128)(2,1)S(1)}, u32[]{:S(2)}, u32[]{:S(2)}) collective-permute-start(bf16[4,2,48,384]{3,2,1,0:T(8,128)(2,1)S(1)} %pad_maximum_fusion.6), channel_id=1, source_target_pairs={{0,32},{1,33},{2,34},{3,35},{4,36},{5,37},{6,38},{7,39},{8,40},{9,... | collective-permute-start | bytes 884744 | tf_op jit(solution)/shard_map/ppermute | solution.py:48
  143.8 14.6 %collective-permute-start.28 = (bf16[4,2,48,384]{3,2,1,0:T(8,128)(2,1)S(1)}, bf16[4,2,48,384]{3,2,1,0:T(8,128)(2,1)S(1)}, u32[]{:S(2)}, u32[]{:S(2)}) collective-permute-start(bf16[4,2,48,384]{3,2,1,0:T(8,128)(2,1)S(1)} %pad_maximum_fusion.6), channel_id=1, source_target_pairs={{0,16},{1,17},{2,18},{3,19},{4,20},{5,21},{6,22},{7,23},{8,24},{9,... | collective-permute-start | bytes 884744 | tf_op jit(solution)/shard_map/ppermute | solution.py:48
  143.8 14.8 %collective-permute-start.33 = (bf16[4,2,48,384]{3,2,1,0:T(8,128)(2,1)S(1)}, bf16[4,2,48,384]{3,2,1,0:T(8,128)(2,1)S(1)}, u32[]{:S(2)}, u32[]{:S(2)}) collective-permute-start(bf16[4,2,48,384]{3,2,1,0:T(8,128)(2,1)S(1)} %pad_maximum_fusion.7), channel_id=1, source_target_pairs={{0,72},{1,73},{2,74},{3,75},{4,76},{5,77},{6,78},{7,79},{8,64},{9,... | collective-permute-start | bytes 884744 | tf_op jit(solution)/shard_map/ppermute | solution.py:48
  144.1 14.6 %collective-permute-start.32 = (bf16[4,2,48,384]{3,2,1,0:T(8,128)(2,1)S(1)}, bf16[4,2,48,384]{3,2,1,0:T(8,128)(2,1)S(1)}, u32[]{:S(2)}, u32[]{:S(2)}) collective-permute-start(bf16[4,2,48,384]{3,2,1,0:T(8,128)(2,1)S(1)} %pad_maximum_fusion.7), channel_id=1, source_target_pairs={{0,8},{1,9},{2,10},{3,11},{4,12},{5,13},{6,14},{7,15},{8,0},{9,1},... | collective-permute-start | bytes 884744 | tf_op jit(solution)/shard_map/ppermute | solution.py:48
  146.6 12.1 %collective-permute-start.31 = (bf16[4,2,48,384]{3,2,1,0:T(8,128)(2,1)S(1)}, bf16[4,2,48,384]{3,2,1,0:T(8,128)(2,1)S(1)}, u32[]{:S(2)}, u32[]{:S(2)}) collective-permute-start(bf16[4,2,48,384]{3,2,1,0:T(8,128)(2,1)S(1)} %pad_maximum_fusion.7), channel_id=1, source_target_pairs={{0,64},{1,65},{2,66},{3,67},{4,68},{5,69},{6,70},{7,71},{8,72},{9,... | collective-permute-start | bytes 884744 | tf_op jit(solution)/shard_map/ppermute | solution.py:48
  158.9 13.6 %copy-start.3 = (bf16[16,2,48,384]{3,2,1,0:T(8,128)(2,1)}, bf16[16,2,48,384]{3,2,1,0:T(8,128)(2,1)S(1)}, u32[]{:S(2)}) copy-start(bf16[16,2,48,384]{3,2,1,0:T(8,128)(2,1)S(1)} %pad_maximum_fusion.3.rest_2_) | copy-start | bytes 3538948
  159.7 10.9 %collective-permute-start.34 = (bf16[16,2,48,384]{3,2,1,0:T(8,128)(2,1)S(1)}, bf16[16,2,48,384]{3,2,1,0:T(8,128)(2,1)S(1)}, u32[]{:S(2)}, u32[]{:S(2)}) collective-permute-start(bf16[16,2,48,384]{3,2,1,0:T(8,128)(2,1)S(1)} %pad_maximum_fusion.2.rest_0_), channel_id=1, source_target_pairs={{0,1},{1,0},{2,3},{3,2},{4,5},{5,4},{6,7},{7,6},{8,9},{9,8},{10,11... | collective-permute-start | bytes 3538952 | tf_op jit(solution)/shard_map/ppermute | solution.py:48
  168.2 4.3 %collective-permute-start.35 = (bf16[16,2,48,384]{3,2,1,0:T(8,128)(2,1)S(1)}, bf16[16,2,48,384]{3,2,1,0:T(8,128)(2,1)}, u32[]{:S(2)}, u32[]{:S(2)}) collective-permute-start(bf16[16,2,48,384]{3,2,1,0:T(8,128)(2,1)S(1)} %pad_maximum_fusion.3.rest_2_), channel_id=1, source_target_pairs={{0,1},{1,0},{2,3},{3,2},{4,5},{5,4},{6,7},{7,6},{8,9},{9,8},{10,11... | collective-permute-start | bytes 3538952 | tf_op jit(solution)/shard_map/ppermute | solution.py:48
  (6 other events, 5.0 us)
where the time goes:
time: 241 us; the launch traced here: 239 us
  Pallas kernels  92.6 us (38%)
  starting transfers between devices  65.9 us (27%)
  blocking collectives  31.1 us (13%)
  waiting for transfers between devices  28.5 us (12%)
  other arithmetic  14.5 us (6%)
  local copies, waits for them, and re-layouts  6.17 us (3%)
    ppermute x36, starting transfers between devices, shifted(): return lax.ppermute(values, AXES, pairs)  57.1 us
    pallas_call x2, Pallas kernels, run_pass(): pl.pallas_call(functools.partial(attend_kernel, turned), grid=(ROWS,), in...  53.5 us
    all_to_all x1, blocking collectives, cross(): return lax.all_to_all(values, AXES, split_axis=0, concat_axis=0, tiled=True)  31.1 us
    ppermute x36, waiting for transfers between devices, shifted(): return lax.ppermute(values, AXES, pairs)  28.5 us
    pallas_call x2, Pallas kernels, project(): pl.pallas_call(functools.partial(project_kernel, crossed), grid=(ROWS,),...  23.8 us
    all_to_all x1, starting transfers between devices, cross(): return lax.all_to_all(values, AXES, split_axis=0, concat_axis=0, tiled=True)  8.74 us
    pallas_call x1, Pallas kernels, add_crossed(): pl.pallas_call(final_kernel, grid=(ROWS,), in_specs=[row_spec, pl.BlockSp...  6.04 us
    pallas_call x1, Pallas kernels, first_bias(): pl.pallas_call(bias_kernel, in_specs=[pl.BlockSpec(memory_space=pltpu.SME...  5.8 us
  transfers between devices with their start and end apart: 37, of which 18 were waited for; matrix products, arithmetic and copies ran while one was open for 3% of the time, Pallas kernels for 11%

commit v1 on v0

--- a/solution.py
+++ b/solution.py
@@ -21,7 +21,7 @@
 CURVE = 4.0
 CODE_STEP = float(np.log(1 + CURVE * 11.32) / 32767)
 AXES = ("row", "col")
-VMEM = 60 * 1024 * 1024
+MIB = 1024 * 1024
 F32, BF16 = jnp.float32, jnp.bfloat16
 NT = (((1,), (1,)), ((), ()))
 NN = (((1,), (0,)), ((), ()))
@@ -73,18 +73,21 @@
         merge_kernel,
         in_specs=[pl.BlockSpec(memory_space=pltpu.SMEM)] + [vmem] * 4,
         out_shape=[jax.ShapeDtypeStruct((2, 48, 384), BF16)] * 2,
-        compiler_params=pltpu.CompilerParams(vmem_limit_bytes=VMEM),
+        compiler_params=pltpu.CompilerParams(vmem_limit_bytes=8 * MIB),
         cost_estimate=pl.CostEstimate(flops=10**7, bytes_accessed=3 * 10**5, transcendentals=0),
     )(scalars, *slots)
 
 
-def gather_plane(place, kept, sent, beside, work):
+def gather_plane(place, kept, sent, beside, work, crossing=False):
     block = jnp.concatenate([kept, shifted(sent, 3, 1)], axis=0)
     slots = [block] + [shifted(block, 1, step) for step in (1, 2, -1)]
+    if crossing:
+        *slots, beside = lax.optimization_barrier((*slots, beside))
+        beside = cross(beside)
     blocks = [ring(pair[None], axis) for pair, axis in zip(merge(place, slots), (0, 2))]
-    *blocks, beside = lax.optimization_barrier((*blocks, beside))
+    blocks, beside = lax.optimization_barrier((blocks, beside))
     blocks = [ring(block, axis) for block, axis in zip(blocks, (2, 0))]
-    *blocks, done = lax.optimization_barrier((*blocks, work(beside)))
+    blocks, done = lax.optimization_barrier((blocks, work(beside)))
     pieces = []
     for block in blocks:
         pieces += [block, shifted(block, 3, 1)]
@@ -139,11 +142,15 @@
     return jnp.where(codes < 0, -size, size)
 
 
-def put_bias(normed, w_bias, rows_ref, row):
+def put_bias(normed, w_bias, rows_ref, step, count):
     bias = dot3(split(w_bias), split(normed), NT)
-    for half in range(2):
-        at = half * 24 + row * 4
-        rows_ref[at : at + 4, :] = bias[:, half * 384 : (half + 1) * 384]
+    for row in range(count):
+
+        @pl.when(step == row)
+        def _():
+            for half in range(2):
+                at = half * 24 + row * 4
+                rows_ref[at : at + 4, :] = bias[:, half * 384 : (half + 1) * 384]
 
 
 def hand_over(scalar_ref, rows_ref, kept_ref, sent_ref):
@@ -153,20 +160,36 @@
 
 
 def bias_kernel(scalar_ref, x_ref, gain_ref, shift_ref, w_ref, kept_ref, sent_ref, rows_ref):
-    for row in range(ROWS):
-        normed = normalize(x_ref[row], gain_ref[0:1, :], shift_ref[0:1, :])
-        put_bias(normed, w_ref[0], rows_ref, row)
-    hand_over(scalar_ref, rows_ref, kept_ref, sent_ref)
+    step = pl.program_id(0)
+    normed = normalize(x_ref[0], gain_ref[0:1, :], shift_ref[0:1, :])
+    put_bias(normed, w_ref[0], rows_ref, step, ROWS)
+
+    @pl.when(step == ROWS - 1)
+    def _():
+        hand_over(scalar_ref, rows_ref, kept_ref, sent_ref)
+
+
+def small(*shape):
+    return pl.BlockSpec(shape, lambda i: (0,) * len(shape))
 
 
 def first_bias(scalars, x, gain, shift, w_bias):
-    vmem = pl.BlockSpec(memory_space=pltpu.VMEM)
     return pl.pallas_call(
         bias_kernel,
-        in_specs=[pl.BlockSpec(memory_space=pltpu.SMEM)] + [vmem] * 4,
+        grid=(ROWS,),
+        in_specs=[
+            pl.BlockSpec(memory_space=pltpu.SMEM),
+            pl.BlockSpec((1, TOKENS, HD), lambda i: (i, 0, 0)),
+            small(2, HD),
+            small(2, HD),
+            small(2, HEADS, HD),
+        ],
+        out_specs=[small(24, 384)] * 2,
         out_shape=[jax.ShapeDtypeStruct((24, 384), BF16)] * 2,
         scratch_shapes=[pltpu.VMEM((48, 384), F32)],
-        compiler_params=pltpu.CompilerParams(vmem_limit_bytes=VMEM),
+        compiler_params=pltpu.CompilerParams(
+            vmem_limit_bytes=24 * MIB, dimension_semantics=("arbitrary",)
+        ),
         cost_estimate=pl.CostEstimate(flops=10**8, bytes_accessed=2 * 10**6, transcendentals=0),
     )(scalars, x, gain, shift, w_bias)
 
@@ -248,7 +271,7 @@
     return pl.pallas_call(
         functools.partial(project_kernel, crossed),
         grid=(ROWS,),
-        in_specs=[whole if crossed else row_spec] + [whole] * 3 + [matrix(crossed)] * 4,
+        in_specs=[whole if crossed else row_spec] + [small(2, HD)] * 3 + [matrix(crossed)] * 4,
         out_specs=[
             head_spec, head_spec, pl.BlockSpec((1, TOKENS, 2 * HD), lambda i: (i, 0, 0)), row_spec,
         ],
@@ -260,7 +283,7 @@
         ],
         scratch_shapes=scratch,
         compiler_params=pltpu.CompilerParams(
-            vmem_limit_bytes=VMEM, dimension_semantics=("arbitrary",)
+            vmem_limit_bytes=24 * MIB, dimension_semantics=("arbitrary",)
         ),
         cost_estimate=pl.CostEstimate(
             flops=10**10, bytes_accessed=17 * 10**6, transcendentals=10**6
@@ -268,7 +291,7 @@
     )(x, *vectors, *matrices)
 
 
-def build_plane(scalar_ref, piece_refs, plane_ref, turned):
+def build_plane(scalar_ref, piece_refs, plane_ref, flat_ref, turned):
     my_x, my_z, core, real = scalar_ref[0], scalar_ref[2], scalar_ref[3], scalar_ref[4]
     limit = ((real + 255) // 256) * 256
 
@@ -280,12 +303,7 @@
         def one_half(own):
             half = core if own else 1 - core
             lanes = pl.ds(pl.multiple_of(half * 384, 128), 384)
-            if turned:
-                key = lax.broadcasted_iota(jnp.int32, (48, 384), 0) + group * 48
-                needed = group * 48 < limit
-            else:
-                key = lax.broadcasted_iota(jnp.int32, (48, 384), 1) + half * 384
-                needed = half * 384 < limit
+            needed = group * 48 < limit if turned else half * 384 < limit
 
             @pl.when(needed)
             def _():
@@ -295,9 +313,13 @@
                     else:
                         at = behind_x * 4 + behind_z
                     values = piece_refs[head // 2 * 2 + (0 if own else 1)][at, head % 2]
-                    plane_ref[head, rows, lanes] = jnp.where(
-                        key < real, values.astype(F32) * LOG2E, NEGATIVE
-                    )
+                    if turned:
+                        flat_ref[head, rows, lanes] = values
+                    else:
+                        key = lax.broadcasted_iota(jnp.int32, (48, 384), 1) + half * 384
+                        plane_ref[head, rows, lanes] = jnp.where(
+                            key < real, values.astype(F32) * LOG2E, NEGATIVE
+                        )
 
         one_half(True)
         one_half(False)
@@ -306,17 +328,16 @@
     lax.fori_loop(0, 16, one_group, 0)
 
     def turn(head, _):
-        for a in range(6):
-
-            @pl.when(a * 128 < limit)
+        for block in range(6):
+            keys = slice(block * 128, block * 128 + 128)
+
+            @pl.when(block * 128 < limit)
             def _():
-                for b in range(a, 6):
-                    aa, bb = slice(a * 128, a * 128 + 128), slice(b * 128, b * 128 + 128)
-                    upper = plane_ref[head, aa, bb]
-                    lower = plane_ref[head, bb, aa]
-                    plane_ref[head, aa, bb] = lower.T
-                    if a != b:
-                        plane_ref[head, bb, aa] = upper.T
+                live = lax.broadcasted_iota(jnp.int32, (128, 128), 1) + block * 128 < real
+                for other in range(6):
+                    rows = slice(other * 128, other * 128 + 128)
+                    values = flat_ref[head, keys, rows].T.astype(F32) * LOG2E
+                    plane_ref[head, rows, keys] = jnp.where(live, values, NEGATIVE)
         return 0
 
     if turned:
@@ -343,14 +364,17 @@
     piece_refs, rest = rest[:4], rest[4:]
     step = pl.program_id(0)
     if turned:
-        crossed_ref, plane_ref, mixed_ref = rest
+        crossed_ref, plane_ref, mixed_ref, flat_ref = rest
     else:
         x_ref, gain_ref, shift_ref, nbias_ref = rest[:4]
-        first_ref, crossed_ref, kept_ref, sent_ref, plane_ref, mixed_ref, rows_ref = rest[4:]
+        first_ref, crossed_ref, kept_ref, sent_ref = rest[4:8]
+        plane_ref, mixed_ref, rows_ref, wide_ref = rest[8:]
 
     @pl.when(step == 0)
     def _():
-        build_plane(scalar_ref, piece_refs, plane_ref, turned)
+        build_plane(scalar_ref, piece_refs, plane_ref, flat_ref if turned else None, turned)
+        if not turned:
+            wide_ref[...] = jnp.zeros_like(wide_ref)
 
     real = scalar_ref[4]
     for keys in (256, 512, 768):
@@ -372,21 +396,15 @@
         standard = standardize(first)
         mixed_ref[...] = encode(standard)
         for column in range(ROWS):
-            crossed_ref[pl.ds(step * ROWS + column, DEVICES, stride=PADDED), :] = mixed_ref[
+            wide_ref[pl.ds(step * ROWS + column, DEVICES, stride=PADDED), :] = mixed_ref[
                 pl.ds(column, DEVICES, stride=ROWS), :
             ]
         normed = standard * gain_ref[1:2, :] + shift_ref[1:2, :]
-        bias = dot3(split(nbias_ref[1]), split(normed), NT)
-        for row in range(ROWS):
-
-            @pl.when(step == row)
-            def _():
-                for half in range(2):
-                    at = half * 24 + row * 4
-                    rows_ref[at : at + 4, :] = bias[:, half * 384 : (half + 1) * 384]
+        put_bias(normed, nbias_ref[1], rows_ref, step, ROWS)
 
         @pl.when(step == ROWS - 1)
         def _():
+            crossed_ref[...] = wide_ref[...].astype(jnp.int32).astype(jnp.int16)
             hand_over(scalar_ref, rows_ref, kept_ref, sent_ref)
 
 
@@ -397,17 +415,19 @@
     in_specs = [pl.BlockSpec(memory_space=pltpu.SMEM), head_spec, head_spec]
     in_specs += [pl.BlockSpec((1, TOKENS, 2 * HD), lambda i: (i, 0, 0)), row_spec]
     in_specs += [matrix(turned)] + [whole] * 4
-    out_shape = [jax.ShapeDtypeStruct((DEVICES * PADDED, HD), F32)]
+    out_shape = [jax.ShapeDtypeStruct((DEVICES * PADDED, HD), F32 if turned else jnp.int16)]
     out_specs = [pl.BlockSpec((DEVICES * PADDED, HD), lambda i: (0, 0))]
     scratch = [pltpu.VMEM((HEADS, TOKENS, TOKENS), F32), pltpu.VMEM((TOKENS, HD), F32)]
+    if turned:
+        scratch.append(pltpu.VMEM((HEADS, TOKENS, TOKENS), BF16))
     args = [scalars, *projected, w_o, *pieces]
     if not turned:
-        in_specs += [row_spec] + [whole] * 3
+        in_specs += [row_spec, small(2, HD), small(2, HD), small(2, HEADS, HD)]
         args += [x, *extra]
         out_shape = [jax.ShapeDtypeStruct((ROWS, TOKENS, HD), F32)] + out_shape
         out_shape += [jax.ShapeDtypeStruct((24, 384), BF16)] * 2
         out_specs = [row_spec] + out_specs + [pl.BlockSpec((24, 384), lambda i: (0, 0))] * 2
-        scratch.append(pltpu.VMEM((48, 384), F32))
+        scratch += [pltpu.VMEM((48, 384), F32), pltpu.VMEM((DEVICES * PADDED, HD), F32)]
     return pl.pallas_call(
         functools.partial(attend_kernel, turned),
         grid=(ROWS,),
@@ -416,7 +436,7 @@
         out_shape=out_shape,
         scratch_shapes=scratch,
         compiler_params=pltpu.CompilerParams(
-            vmem_limit_bytes=VMEM, dimension_semantics=("arbitrary",)
+            vmem_limit_bytes=26 * MIB, dimension_semantics=("arbitrary",)
         ),
         cost_estimate=pl.CostEstimate(
             flops=2 * 10**10, bytes_accessed=2 * 10**7, transcendentals=14 * 10**6
@@ -443,7 +463,7 @@
         out_shape=jax.ShapeDtypeStruct((ROWS, TOKENS, HD), F32),
         scratch_shapes=[pltpu.VMEM((TOKENS, HD), F32)],
         compiler_params=pltpu.CompilerParams(
-            vmem_limit_bytes=VMEM, dimension_semantics=("arbitrary",)
+            vmem_limit_bytes=16 * MIB, dimension_semantics=("arbitrary",)
         ),
         cost_estimate=pl.CostEstimate(flops=10**6, bytes_accessed=8 * 10**6, transcendentals=0),
     )(first, update)
@@ -472,16 +492,16 @@
     vectors, matrices = (ln_gain, ln_shift, gate_shift), (w_query, w_key, w_value, w_gate)
 
     start = first_bias(place, pair_tensor, ln_gain, ln_shift, w_bias)
-    planes, projected = gather_plane(
-        place, *start, pair_tensor, lambda cells: project(False, cells, vectors, matrices)
+    scalars = jnp.concatenate([place, jnp.sum(token_mask, dtype=jnp.int32, keepdims=True)])
+    planes, (projected, scalars) = gather_plane(
+        place, *start, (pair_tensor, scalars),
+        lambda held: (project(False, held[0], vectors, matrices), held[1]),
     )
-    scalars = jnp.concatenate([place, jnp.sum(token_mask, dtype=jnp.int32, keepdims=True)])
     first, codes, *end = run_pass(
         False, scalars, projected, w_out, planes, pair_tensor, (ln_gain, ln_shift, w_bias)
     )
-    codes = cross(codes.astype(jnp.int16))
     planes, projected = gather_plane(
-        place, *end, codes, lambda held: project(True, held.astype(F32), vectors, matrices)
+        place, *end, codes, lambda held: project(True, held.astype(F32), vectors, matrices), True
     )
     (update,) = run_pass(True, scalars, projected, w_out, planes)
     return add_crossed(first, cross(update.astype(jnp.float16)).astype(F32))

time: 241 us -> 228 us (0.946); the launches traced: 239 us -> 230 us
  waiting for transfers between devices: 28.5 us -> 43 us
  other arithmetic: 14.5 us -> 4.53 us
  starting transfers between devices: 65.9 us -> 58.6 us
  Pallas kernels: 92.6 us -> 88.3 us
    ppermute x36, waiting for transfers between devices: 28.5 us -> 43 us  [shifted(): return lax.ppermute(values, AXES, pairs)]
    ppermute x36, starting transfers between devices: 57.1 us -> 48.1 us  [shifted(): return lax.ppermute(values, AXES, pairs)]
    pallas_call x2, Pallas kernels: 53.5 us -> 60.3 us  [run_pass(): pl.pallas_call(functools.partial(attend_kernel, turned), grid=(ROWS,), in...]
    pallas_call x2, Pallas kernels: 23.8 us -> 18.4 us  [project(): pl.pallas_call(functools.partial(project_kernel, crossed), grid=(ROWS,),...]
    pallas_call x1, Pallas kernels: 6.04 us -> 2.74 us  [add_crossed(): pl.pallas_call(final_kernel, grid=(ROWS,), in_specs=[row_spec, pl.BlockSp...]
    convert_element_type x1 -> x0, other arithmetic: 3.26 us -> none  [on_device(): codes = cross(codes.astype(jnp.int16))]
    convert_element_type x2, other arithmetic: 3.63 us -> 0.43 us  [on_device(): return add_crossed(first, cross(update.astype(jnp.float16)).astype(F32))]
    concatenate x8, other arithmetic: 4.49 us -> 1.66 us  [ring(): jnp.concatenate([block, shifted(block, axis, 1), shifted(block, axis, 2),...]
  transfers between devices with their start and end apart: 37 -> 37, of which waited for: 18 -> 19; matrix products, arithmetic and copies ran while one was open for 3% -> 2% of each run, Pallas kernels for 11% -> 8%
where the time goes in v1:
time: 228 us; the launch traced here: 230 us
  Pallas kernels  88.3 us (39%)
  starting transfers between devices  58.6 us (26%)
  waiting for transfers between devices  43 us (19%)
  blocking collectives  29.2 us (13%)
  local copies, waits for them, and re-layouts  5.63 us (2%)
  other arithmetic  4.53 us (2%)
    pallas_call x2, Pallas kernels, run_pass(): pl.pallas_call(functools.partial(attend_kernel, turned), grid=(ROWS,), in...  60.3 us
    ppermute x36, starting transfers between devices, shifted(): return lax.ppermute(values, AXES, pairs)  48.1 us
    ppermute x36, waiting for transfers between devices, shifted(): return lax.ppermute(values, AXES, pairs)  43 us
    all_to_all x1, blocking collectives, cross(): return lax.all_to_all(values, AXES, split_axis=0, concat_axis=0, tiled=True)  29.2 us
    pallas_call x2, Pallas kernels, project(): pl.pallas_call(functools.partial(project_kernel, crossed), grid=(ROWS,),...  18.4 us
    all_to_all x1, starting transfers between devices, cross(): return lax.all_to_all(values, AXES, split_axis=0, concat_axis=0, tiled=True)  10.5 us
    pallas_call x1, Pallas kernels, first_bias(): pl.pallas_call(bias_kernel, grid=(ROWS,), in_specs=[pl.BlockSpec(memory_s...  5.2 us
    unnamed x38, local copies, waits for them, and re-layouts  4.84 us
  transfers between devices with their start and end apart: 37, of which 19 were waited for; matrix products, arithmetic and copies ran while one was open for 2% of the time, Pallas kernels for 8%

profile of v1, /device:TPU:1, one launch (start us, length us, event | category | flops | bytes accessed | tf_op | source)
XLA Modules:
  0.0 230.1 jit_solution(7479203056683577523)
XLA Ops:
  0.1 1.7 copy-done
  3.8 5.2 %shard_map.109 = (bf16[24,384]{1,0:T(8,128)(2,1)S(1)}, bf16[24,384]{1,0:T(8,128)(2,1)S(1)}) custom-call(s32[4]{0:T(128)S(1)} %pad_add_fusion.scalar_ref, f32[6,768,128]{2,1,0:T(8,128)S(1)} %copy-done, f32[2,128]{1,0:T(2,128)S(1)} %copy-done.6, f32[2,128]{1,0:T(2,128)S(1)} %copy-done.8, f32[2,4,128]{2,1,0:T(4,128)S(1)} %copy-done.4), custom_call_target="tpu_custom_call" | custom-call | flops 100000000 | bytes 2000000 | tf_op jit(solution)/shard_map/pallas_call | solution.py:177
  9.1 1.5 collective-permute-start
  10.6 0.8 collective-permute-done
  11.4 2.8 %collective-permute-start.3 = (bf16[48,384]{1,0:T(8,128)(2,1)S(1)}, bf16[48,384]{1,0:T(8,128)(2,1)S(1)}, u32[]{:S(2)}, u32[]{:S(2)}) collective-permute-start(bf16[48,384]{1,0:T(8,128)(2,1)S(1)} %constant_dynamic-update-slice_fusion.refs_0_), channel_id=1, source_target_pairs={{0,6},{1,7},{2,0},{3,1},{4,2},{5,3},{6,4},{7,5},{8,14},{9,15},{10,... | collective-permute-start | bytes 110600 | tf_op jit(solution)/shard_map/ppermute | solution.py:48
  15.3 3.3 %collective-permute-done.2.refs_2_ = bf16[48,384]{1,0:T(8,128)(2,1)S(1)} collective-permute-done((bf16[48,384]{1,0:T(8,128)(2,1)S(1)}, bf16[48,384]{1,0:T(8,128)(2,1)S(1)}, u32[]{:S(2)}, u32[]{:S(2)}) %collective-permute-start.2) | collective-permute-done | bytes 36896 | tf_op jit(solution)/shard_map/ppermute | solution.py:48
  19.0 0.8 shard_map.110
  19.8 3.8 %collective-permute-start.9 = (bf16[1,2,48,384]{3,2,1,0:T(8,128)(2,1)S(1)}, bf16[1,2,48,384]{3,2,1,0:T(8,128)(2,1)S(1)}, u32[]{:S(2)}, u32[]{:S(2)}) collective-permute-start(bf16[1,2,48,384]{3,2,1,0:T(8,128)(2,1)S(1)} %bitcast.24), channel_id=1, source_target_pairs={{0,48},{1,49},{2,50},{3,51},{4,52},{5,53},{6,54},{7,55},{8,56},{9,... | collective-permute-start | bytes 221192 | tf_op jit(solution)/shard_map/ppermute | solution.py:48
  25.0 0.8 concatenate.37.scalar_ref
  25.8 2.5 %collective-permute-start.6 = (bf16[1,2,48,384]{3,2,1,0:T(8,128)(2,1)S(1)}, bf16[1,2,48,384]{3,2,1,0:T(8,128)(2,1)S(1)}, u32[]{:S(2)}, u32[]{:S(2)}) collective-permute-start(bf16[1,2,48,384]{3,2,1,0:T(8,128)(2,1)S(1)} %bitcast.16), channel_id=1, source_target_pairs={{0,72},{1,73},{2,74},{3,75},{4,76},{5,77},{6,78},{7,79},{8,64},{9,... | collective-permute-start | bytes 221192 | tf_op jit(solution)/shard_map/ppermute | solution.py:48
  29.7 3.4 %collective-permute-done.5 = bf16[1,2,48,384]{3,2,1,0:T(8,128)(2,1)S(1)} collective-permute-done((bf16[1,2,48,384]{3,2,1,0:T(8,128)(2,1)S(1)}, bf16[1,2,48,384]{3,2,1,0:T(8,128)(2,1)S(1)}, u32[]{:S(2)}, u32[]{:S(2)}) %collective-permute-start.5) | collective-permute-done | bytes 73760 | tf_op jit(solution)/shard_map/ppermute | solution.py:48
  33.0 0.7 collective-permute-done.4
  33.8 2.0 collective-permute-start.12
  35.9 1.8 collective-permute-start.11
  37.9 0.8 collective-permute-start.14
  38.7 1.2 collective-permute-done.12
  40.0 10.2 %shard_map.111 = (bf16[6,4,768,128]{3,2,1,0:T(8,128)(2,1)S(1)}, bf16[6,4,768,128]{3,2,1,0:T(8,128)(2,1)S(1)}, bf16[6,768,256]{2,1,0:T(8,128)(2,1)S(1)}, f32[6,768,128]{2,1,0:T(8,128)S(1)}) custom-call(f32[6,768,128]{2,1,0:T(8,128)S(1)} %copy-done.1, f32[2,128]{1,0:T(2,128)S(1)} %copy-done.7, f32[2,128]{1,0:T(2,128)S(1)} %copy-done.9, ...), custom_call_target="tpu_custom_call" | custom-call | flops 10000000000 | bytes 17000000 | tf_op jit(solution)/shard_map/pallas_call | solution.py:271
  50.7 9.1 %collective-permute-start.16 = (bf16[16,2,48,384]{3,2,1,0:T(8,128)(2,1)S(1)}, bf16[16,2,48,384]{3,2,1,0:T(8,128)(2,1)S(1)}, u32[]{:S(2)}, u32[]{:S(2)}) collective-permute-start(bf16[16,2,48,384]{3,2,1,0:T(8,128)(2,1)S(1)} %pad_maximum_fusion.rest_0_), channel_id=1, source_target_pairs={{0,1},{1,0},{2,3},{3,2},{4,5},{5,4},{6,7},{7,6},{8,9},{9,8},{10,11... | collective-permute-start | bytes 3538952 | tf_op jit(solution)/shard_map/ppermute | solution.py:48
  60.2 2.2 collective-permute-done.16.rest_1_
  62.4 1.7 collective-permute-done.17.rest_3_
  64.1 31.8 %shard_map.112 = (f32[6,768,128]{2,1,0:T(8,128)S(1)}, s16[5120,128]{1,0:T(8,128)(2,1)S(1)}, bf16[24,384]{1,0:T(8,128)(2,1)S(1)}, bf16[24,384]{1,0:T(8,128)(2,1)S(1)}) custom-call(s32[5]{0:T(128)S(1)} %concatenate.37.scalar_ref, bf16[6,4,768,128]{3,2,1,0:T(8,128)(2,1)S(1)} %get-tuple-element.61.q_ref, bf16[6,4,768,128]{3,2,1,0:T(8,128)(2,1)S(1)} %get-tuple-element.62.k_ref, ...), custom_call_target="tpu_custom_call" | custom-call | flops 20000000000 | bytes 20000000 | tf_op jit(solution)/shard_map/pallas_call | solution.py:431
  95.9 1.0 copy-done.3
  97.4 0.8 collective-permute-done.18
  98.2 1.0 collective-permute-start.21
  99.2 0.9 collective-permute-start.20
  100.1 0.8 collective-permute-start.19
  101.0 2.5 %collective-permute-done.20.refs_2_ = bf16[48,384]{1,0:T(8,128)(2,1)S(1)} collective-permute-done((bf16[48,384]{1,0:T(8,128)(2,1)S(1)}, bf16[48,384]{1,0:T(8,128)(2,1)S(1)}, u32[]{:S(2)}, u32[]{:S(2)}) %collective-permute-start.20) | collective-permute-done | bytes 36896 | tf_op jit(solution)/shard_map/ppermute | solution.py:48
  104.2 10.5 %all-to-all-start = ((s16[128,40,128]{2,1,0:T(8,128)(2,1)}), s16[128,40,128]{2,1,0:T(8,128)(2,1)}, u32[]{:S(2)}, u32[]{:S(2)}) async-start(s16[128,40,128]{2,1,0:T(8,128)(2,1)} %bitcast.15), calls=%async_computation | async-start | bytes 2621440 | tf_op jit(solution)/shard_map/all_to_all | solution.py:473
  114.7 0.8 shard_map.113
  115.5 3.3 %collective-permute-start.27 = (bf16[1,2,48,384]{3,2,1,0:T(8,128)(2,1)S(1)}, bf16[1,2,48,384]{3,2,1,0:T(8,128)(2,1)S(1)}, u32[]{:S(2)}, u32[]{:S(2)}) collective-permute-start(bf16[1,2,48,384]{3,2,1,0:T(8,128)(2,1)S(1)} %bitcast.28), channel_id=1, source_target_pairs={{0,48},{1,49},{2,50},{3,51},{4,52},{5,53},{6,54},{7,55},{8,56},{9,... | collective-permute-start | bytes 221192 | tf_op jit(solution)/shard_map/ppermute | solution.py:48
  119.0 0.8 collective-permute-start.25
  119.7 2.6 %collective-permute-start.24 = (bf16[1,2,48,384]{3,2,1,0:T(8,128)(2,1)S(1)}, bf16[1,2,48,384]{3,2,1,0:T(8,128)(2,1)S(1)}, u32[]{:S(2)}, u32[]{:S(2)}) collective-permute-start(bf16[1,2,48,384]{3,2,1,0:T(8,128)(2,1)S(1)} %bitcast.20), channel_id=1, source_target_pairs={{0,72},{1,73},{2,74},{3,75},{4,76},{5,77},{6,78},{7,79},{8,64},{9,... | collective-permute-start | bytes 221192 | tf_op jit(solution)/shard_map/ppermute | solution.py:48
  122.9 8.8 %collective-permute-done.27 = bf16[1,2,48,384]{3,2,1,0:T(8,128)(2,1)S(1)} collective-permute-done((bf16[1,2,48,384]{3,2,1,0:T(8,128)(2,1)S(1)}, bf16[1,2,48,384]{3,2,1,0:T(8,128)(2,1)S(1)}, u32[]{:S(2)}, u32[]{:S(2)}) %collective-permute-start.27) | collective-permute-done | bytes 73760 | tf_op jit(solution)/shard_map/ppermute | solution.py:48
  131.7 1.4 collective-permute-start.22
  133.1 1.0 collective-permute-done.26
  134.1 2.5 %collective-permute-done.25 = bf16[1,2,48,384]{3,2,1,0:T(8,128)(2,1)S(1)} collective-permute-done((bf16[1,2,48,384]{3,2,1,0:T(8,128)(2,1)S(1)}, bf16[1,2,48,384]{3,2,1,0:T(8,128)(2,1)S(1)}, u32[]{:S(2)}, u32[]{:S(2)}) %collective-permute-start.25) | collective-permute-done | bytes 73760 | tf_op jit(solution)/shard_map/ppermute | solution.py:48
  136.7 0.8 pad_maximum_fusion.6
  137.4 4.3 %collective-permute-start.30 = (bf16[4,2,48,384]{3,2,1,0:T(8,128)(2,1)}, bf16[4,2,48,384]{3,2,1,0:T(8,128)(2,1)S(1)}, u32[]{:S(2)}, u32[]{:S(2)}) collective-permute-start(bf16[4,2,48,384]{3,2,1,0:T(8,128)(2,1)} %pad_maximum_fusion.6), channel_id=1, source_target_pairs={{0,48},{1,49},{2,50},{3,51},{4,52},{5,53},{6,54},{7,55},{8,56},{9,... | collective-permute-start | bytes 884744 | tf_op jit(solution)/shard_map/ppermute | solution.py:48
  142.4 0.8 collective-permute-start.32
  143.2 1.7 convert_element_type.11.x_ref
  144.9 8.9 %collective-permute-done.30 = bf16[4,2,48,384]{3,2,1,0:T(8,128)(2,1)S(1)} collective-permute-done((bf16[4,2,48,384]{3,2,1,0:T(8,128)(2,1)}, bf16[4,2,48,384]{3,2,1,0:T(8,128)(2,1)S(1)}, u32[]{:S(2)}, u32[]{:S(2)}) %collective-permute-start.30) | collective-permute-done | bytes 294944 | tf_op jit(solution)/shard_map/ppermute | solution.py:48
  153.8 8.2 %shard_map.114 = (bf16[6,4,768,128]{3,2,1,0:T(8,128)(2,1)S(1)}, bf16[6,4,768,128]{3,2,1,0:T(8,128)(2,1)S(1)}, bf16[6,768,256]{2,1,0:T(8,128)(2,1)S(1)}, f32[6,768,128]{2,1,0:T(8,128)S(1)}) custom-call(f32[5120,128]{1,0:T(8,128)S(1)} %convert_element_type.11.x_ref, f32[2,128]{1,0:T(2,128)S(1)} %copy-done.7, f32[2,128]{1,0:T(2,128)S(1)} %copy-done.9, ...), custom_call_target="tpu_custom_call" | custom-call | flops 10000000000 | bytes 17000000 | tf_op jit(solution)/shard_map/pallas_call | solution.py:271
  162.5 2.2 collective-permute-start.34
  165.1 2.1 collective-permute-done.34.rest_1_
  167.2 1.7 collective-permute-done.35.rest_3_
  168.9 28.4 %shard_map.115 = f32[5120,128]{1,0:T(8,128)S(1)} custom-call(s32[5]{0:T(128)S(1)} %concatenate.37.scalar_ref, bf16[6,4,768,128]{3,2,1,0:T(8,128)(2,1)S(1)} %get-tuple-element.85.q_ref, bf16[6,4,768,128]{3,2,1,0:T(8,128)(2,1)S(1)} %get-tuple-element.86.k_ref, bf16[6,768,256]{2,1,0:T(8,128)(2,1)S(1)} %get-tuple-element.87.v_ref, ...), custom_call_target="tpu_custom_call" | custom-call | flops 20000000000 | bytes 20000000 | tf_op jit(solution)/shard_map/pallas_call | solution.py:431
  197.5 29.2 %all_to_all.21 = f16[128,40,128]{2,1,0:T(8,128)(2,1)S(1)} all-to-all(f16[128,40,128]{2,1,0:T(8,128)(2,1)S(1)} %bitcast.32), channel_id=1, replica_groups=mesh['row'=8,'col'=16] {'row','col'}, dimensions={0} | all-to-all | bytes 2621440 | tf_op jit(solution)/shard_map/all_to_all | solution.py:473
  226.9 2.7 %shard_map.116 = f32[6,768,128]{2,1,0:T(8,128)} custom-call(f32[6,768,128]{2,1,0:T(8,128)S(1)} %get-tuple-element.67.first_ref, f32[5120,128]{1,0:T(8,128)S(1)} %bitcast_convert_fusion.update_ref), custom_call_target="tpu_custom_call" | custom-call | flops 1000000 | bytes 8000000 | tf_op jit(solution)/shard_map/pallas_call | solution.py:458
  (89 shorter events, 11.2 us)
Async XLA Ops:
  3.8 20.5 %copy-start.17 = (s32[768]{0:T(1024)S(1)}, s32[768]{0:T(1024)}, u32[]{:S(2)}) copy-start(s32[768]{0:T(1024)} %param.12) | copy-start | bytes 9220
  3.8 36.2 %copy-start.1 = (f32[6,768,128]{2,1,0:T(8,128)S(1)}, f32[6,768,128]{2,1,0:T(8,128)}, u32[]{:S(2)}) copy-start(f32[6,768,128]{2,1,0:T(8,128)} %rest_4_.1) | copy-start | bytes 7077892
  9.0 31.0 %copy-start.7 = (f32[2,128]{1,0:T(2,128)S(1)}, f32[2,128]{1,0:T(2,128)}, u32[]{:S(2)}) copy-start(f32[2,128]{1,0:T(2,128)} %gain_ref.5) | copy-start | bytes 3076
  9.0 31.0 %copy-start.9 = (f32[2,128]{1,0:T(2,128)S(1)}, f32[2,128]{1,0:T(2,128)}, u32[]{:S(2)}) copy-start(f32[2,128]{1,0:T(2,128)} %shift_ref.5) | copy-start | bytes 3076
  9.0 31.0 %copy-start.10 = (f32[2,128,128]{2,1,0:T(8,128)S(1)}, f32[2,128,128]{2,1,0:T(8,128)}, u32[]{:S(2)}) copy-start(f32[2,128,128]{2,1,0:T(8,128)} %wq_ref.3) | copy-start | bytes 393220
  9.0 31.0 %copy-start.11 = (f32[2,128,128]{2,1,0:T(8,128)S(1)}, f32[2,128,128]{2,1,0:T(8,128)}, u32[]{:S(2)}) copy-start(f32[2,128,128]{2,1,0:T(8,128)} %wk_ref.3) | copy-start | bytes 393220
  9.0 31.0 %copy-start.12 = (f32[2,128,128]{2,1,0:T(8,128)S(1)}, f32[2,128,128]{2,1,0:T(8,128)}, u32[]{:S(2)}) copy-start(f32[2,128,128]{2,1,0:T(8,128)} %wv_ref.3) | copy-start | bytes 393220
  9.1 31.0 %copy-start.13 = (f32[2,128,128]{2,1,0:T(8,128)S(1)}, f32[2,128,128]{2,1,0:T(8,128)}, u32[]{:S(2)}) copy-start(f32[2,128,128]{2,1,0:T(8,128)} %wg_ref.3) | copy-start | bytes 393220
  9.1 31.0 %copy-start.15 = (f32[2,128]{1,0:T(2,128)S(1)}, f32[2,128]{1,0:T(2,128)}, u32[]{:S(2)}) copy-start(f32[2,128]{1,0:T(2,128)} %gs_ref.3) | copy-start | bytes 3076
  9.1 2.3 %collective-permute-start = (bf16[24,384]{1,0:T(8,128)(2,1)S(1)}, bf16[24,384]{1,0:T(8,128)(2,1)S(1)}, u32[]{:S(2)}, u32[]{:S(2)}) collective-permute-start(bf16[24,384]{1,0:T(8,128)(2,1)S(1)} %get-tuple-element.49), channel_id=1, source_target_pairs={{0,1},{1,0},{2,3},{3,2},{4,5},{5,4},{6,7},{7,6},{8,9},{9,8},{10,11... | collective-permute-start | bytes 55304 | tf_op jit(solution)/shard_map/ppermute | solution.py:48
  11.4 3.9 %collective-permute-start.3 = (bf16[48,384]{1,0:T(8,128)(2,1)S(1)}, bf16[48,384]{1,0:T(8,128)(2,1)S(1)}, u32[]{:S(2)}, u32[]{:S(2)}) collective-permute-start(bf16[48,384]{1,0:T(8,128)(2,1)S(1)} %constant_dynamic-update-slice_fusion.refs_0_), channel_id=1, source_target_pairs={{0,6},{1,7},{2,0},{3,1},{4,2},{5,3},{6,4},{7,5},{8,14},{9,15},{10,... | collective-permute-start | bytes 110600 | tf_op jit(solution)/shard_map/ppermute | solution.py:48
  14.3 4.3 %collective-permute-start.2 = (bf16[48,384]{1,0:T(8,128)(2,1)S(1)}, bf16[48,384]{1,0:T(8,128)(2,1)S(1)}, u32[]{:S(2)}, u32[]{:S(2)}) collective-permute-start(bf16[48,384]{1,0:T(8,128)(2,1)S(1)} %constant_dynamic-update-slice_fusion.refs_0_), channel_id=1, source_target_pairs={{0,4},{1,5},{2,6},{3,7},{4,0},{5,1},{6,2},{7,3},{8,12},{9,13},{10,... | collective-permute-start | bytes 110600 | tf_op jit(solution)/shard_map/ppermute | solution.py:48
  14.6 4.4 %collective-permute-start.1 = (bf16[48,384]{1,0:T(8,128)(2,1)S(1)}, bf16[48,384]{1,0:T(8,128)(2,1)S(1)}, u32[]{:S(2)}, u32[]{:S(2)}) collective-permute-start(bf16[48,384]{1,0:T(8,128)(2,1)S(1)} %constant_dynamic-update-slice_fusion.refs_0_), channel_id=1, source_target_pairs={{0,2},{1,3},{2,4},{3,5},{4,6},{5,7},{6,0},{7,1},{8,10},{9,11},{10,... | collective-permute-start | bytes 110600 | tf_op jit(solution)/shard_map/ppermute | solution.py:48
  19.8 9.0 %collective-permute-start.9 = (bf16[1,2,48,384]{3,2,1,0:T(8,128)(2,1)S(1)}, bf16[1,2,48,384]{3,2,1,0:T(8,128)(2,1)S(1)}, u32[]{:S(2)}, u32[]{:S(2)}) collective-permute-start(bf16[1,2,48,384]{3,2,1,0:T(8,128)(2,1)S(1)} %bitcast.24), channel_id=1, source_target_pairs={{0,48},{1,49},{2,50},{3,51},{4,52},{5,53},{6,54},{7,55},{8,56},{9,... | collective-permute-start | bytes 221192 | tf_op jit(solution)/shard_map/ppermute | solution.py:48
  23.6 5.8 %collective-permute-start.8 = (bf16[1,2,48,384]{3,2,1,0:T(8,128)(2,1)S(1)}, bf16[1,2,48,384]{3,2,1,0:T(8,128)(2,1)S(1)}, u32[]{:S(2)}, u32[]{:S(2)}) collective-permute-start(bf16[1,2,48,384]{3,2,1,0:T(8,128)(2,1)S(1)} %bitcast.25), channel_id=1, source_target_pairs={{0,32},{1,33},{2,34},{3,35},{4,36},{5,37},{6,38},{7,39},{8,40},{9,... | collective-permute-start | bytes 221192 | tf_op jit(solution)/shard_map/ppermute | solution.py:48
  23.6 5.8 %collective-permute-start.7 = (bf16[1,2,48,384]{3,2,1,0:T(8,128)(2,1)S(1)}, bf16[1,2,48,384]{3,2,1,0:T(8,128)(2,1)S(1)}, u32[]{:S(2)}, u32[]{:S(2)}) collective-permute-start(bf16[1,2,48,384]{3,2,1,0:T(8,128)(2,1)S(1)} %bitcast.26), channel_id=1, source_target_pairs={{0,16},{1,17},{2,18},{3,19},{4,20},{5,21},{6,22},{7,23},{8,24},{9,... | collective-permute-start | bytes 221192 | tf_op jit(solution)/shard_map/ppermute | solution.py:48
  25.8 3.9 %collective-permute-start.6 = (bf16[1,2,48,384]{3,2,1,0:T(8,128)(2,1)S(1)}, bf16[1,2,48,384]{3,2,1,0:T(8,128)(2,1)S(1)}, u32[]{:S(2)}, u32[]{:S(2)}) collective-permute-start(bf16[1,2,48,384]{3,2,1,0:T(8,128)(2,1)S(1)} %bitcast.16), channel_id=1, source_target_pairs={{0,72},{1,73},{2,74},{3,75},{4,76},{5,77},{6,78},{7,79},{8,64},{9,... | collective-permute-start | bytes 221192 | tf_op jit(solution)/shard_map/ppermute | solution.py:48
  28.3 4.8 %collective-permute-start.5 = (bf16[1,2,48,384]{3,2,1,0:T(8,128)(2,1)S(1)}, bf16[1,2,48,384]{3,2,1,0:T(8,128)(2,1)S(1)}, u32[]{:S(2)}, u32[]{:S(2)}) collective-permute-start(bf16[1,2,48,384]{3,2,1,0:T(8,128)(2,1)S(1)} %bitcast.17), channel_id=1, source_target_pairs={{0,8},{1,9},{2,10},{3,11},{4,12},{5,13},{6,14},{7,15},{8,0},{9,1},... | collective-permute-start | bytes 221192 | tf_op jit(solution)/shard_map/ppermute | solution.py:48
  28.8 5.0 %collective-permute-start.4 = (bf16[1,2,48,384]{3,2,1,0:T(8,128)(2,1)S(1)}, bf16[1,2,48,384]{3,2,1,0:T(8,128)(2,1)S(1)}, u32[]{:S(2)}, u32[]{:S(2)}) collective-permute-start(bf16[1,2,48,384]{3,2,1,0:T(8,128)(2,1)S(1)} %bitcast.18), channel_id=1, source_target_pairs={{0,64},{1,65},{2,66},{3,67},{4,68},{5,69},{6,70},{7,71},{8,72},{9,... | collective-permute-start | bytes 221192 | tf_op jit(solution)/shard_map/ppermute | solution.py:48
  33.8 6.1 %collective-permute-start.12 = (bf16[4,2,48,384]{3,2,1,0:T(8,128)(2,1)S(1)}, bf16[4,2,48,384]{3,2,1,0:T(8,128)(2,1)S(1)}, u32[]{:S(2)}, u32[]{:S(2)}) collective-permute-start(bf16[4,2,48,384]{3,2,1,0:T(8,128)(2,1)S(1)} %pad_maximum_fusion.4), channel_id=1, source_target_pairs={{0,48},{1,49},{2,50},{3,51},{4,52},{5,53},{6,54},{7,55},{8,56},{9,... | collective-permute-start | bytes 884744 | tf_op jit(solution)/shard_map/ppermute | solution.py:48
  35.9 14.4 %collective-permute-start.11 = (bf16[4,2,48,384]{3,2,1,0:T(8,128)(2,1)S(1)}, bf16[4,2,48,384]{3,2,1,0:T(8,128)(2,1)S(1)}, u32[]{:S(2)}, u32[]{:S(2)}) collective-permute-start(bf16[4,2,48,384]{3,2,1,0:T(8,128)(2,1)S(1)} %pad_maximum_fusion.4), channel_id=1, source_target_pairs={{0,32},{1,33},{2,34},{3,35},{4,36},{5,37},{6,38},{7,39},{8,40},{9,... | collective-permute-start | bytes 884744 | tf_op jit(solution)/shard_map/ppermute | solution.py:48
  37.6 12.6 %collective-permute-start.10 = (bf16[4,2,48,384]{3,2,1,0:T(8,128)(2,1)S(1)}, bf16[4,2,48,384]{3,2,1,0:T(8,128)(2,1)S(1)}, u32[]{:S(2)}, u32[]{:S(2)}) collective-permute-start(bf16[4,2,48,384]{3,2,1,0:T(8,128)(2,1)S(1)} %pad_maximum_fusion.4), channel_id=1, source_target_pairs={{0,16},{1,17},{2,18},{3,19},{4,20},{5,21},{6,22},{7,23},{8,24},{9,... | collective-permute-start | bytes 884744 | tf_op jit(solution)/shard_map/ppermute | solution.py:48
  37.6 12.9 %collective-permute-start.15 = (bf16[4,2,48,384]{3,2,1,0:T(8,128)(2,1)S(1)}, bf16[4,2,48,384]{3,2,1,0:T(8,128)(2,1)S(1)}, u32[]{:S(2)}, u32[]{:S(2)}) collective-permute-start(bf16[4,2,48,384]{3,2,1,0:T(8,128)(2,1)S(1)} %pad_maximum_fusion.5), channel_id=1, source_target_pairs={{0,72},{1,73},{2,74},{3,75},{4,76},{5,77},{6,78},{7,79},{8,64},{9,... | collective-permute-start | bytes 884744 | tf_op jit(solution)/shard_map/ppermute | solution.py:48
  37.9 12.6 %collective-permute-start.14 = (bf16[4,2,48,384]{3,2,1,0:T(8,128)(2,1)S(1)}, bf16[4,2,48,384]{3,2,1,0:T(8,128)(2,1)S(1)}, u32[]{:S(2)}, u32[]{:S(2)}) collective-permute-start(bf16[4,2,48,384]{3,2,1,0:T(8,128)(2,1)S(1)} %pad_maximum_fusion.5), channel_id=1, source_target_pairs={{0,8},{1,9},{2,10},{3,11},{4,12},{5,13},{6,14},{7,15},{8,0},{9,1},... | collective-permute-start | bytes 884744 | tf_op jit(solution)/shard_map/ppermute | solution.py:48
  40.0 10.6 %collective-permute-start.13 = (bf16[4,2,48,384]{3,2,1,0:T(8,128)(2,1)S(1)}, bf16[4,2,48,384]{3,2,1,0:T(8,128)(2,1)S(1)}, u32[]{:S(2)}, u32[]{:S(2)}) collective-permute-start(bf16[4,2,48,384]{3,2,1,0:T(8,128)(2,1)S(1)} %pad_maximum_fusion.5), channel_id=1, source_target_pairs={{0,64},{1,65},{2,66},{3,67},{4,68},{5,69},{6,70},{7,71},{8,72},{9,... | collective-permute-start | bytes 884744 | tf_op jit(solution)/shard_map/ppermute | solution.py:48
  50.3 13.8 %copy-start.14 = (f32[2,128,128]{2,1,0:T(8,128)S(1)}, f32[2,128,128]{2,1,0:T(8,128)}, u32[]{:S(2)}) copy-start(f32[2,128,128]{2,1,0:T(8,128)} %wo_ref.3) | copy-start | bytes 393220
  50.7 11.6 %collective-permute-start.16 = (bf16[16,2,48,384]{3,2,1,0:T(8,128)(2,1)S(1)}, bf16[16,2,48,384]{3,2,1,0:T(8,128)(2,1)S(1)}, u32[]{:S(2)}, u32[]{:S(2)}) collective-permute-start(bf16[16,2,48,384]{3,2,1,0:T(8,128)(2,1)S(1)} %pad_maximum_fusion.rest_0_), channel_id=1, source_target_pairs={{0,1},{1,0},{2,3},{3,2},{4,5},{5,4},{6,7},{7,6},{8,9},{9,8},{10,11... | collective-permute-start | bytes 3538952 | tf_op jit(solution)/shard_map/ppermute | solution.py:48
  59.9 4.2 %collective-permute-start.17 = (bf16[16,2,48,384]{3,2,1,0:T(8,128)(2,1)S(1)}, bf16[16,2,48,384]{3,2,1,0:T(8,128)(2,1)S(1)}, u32[]{:S(2)}, u32[]{:S(2)}) collective-permute-start(bf16[16,2,48,384]{3,2,1,0:T(8,128)(2,1)S(1)} %pad_maximum_fusion.1.rest_2_), channel_id=1, source_target_pairs={{0,1},{1,0},{2,3},{3,2},{4,5},{5,4},{6,7},{7,6},{8,9},{9,8},{10,11... | collective-permute-start | bytes 3538952 | tf_op jit(solution)/shard_map/ppermute | solution.py:48
  97.0 1.2 collective-permute-start.18
  98.2 2.8 %collective-permute-start.21 = (bf16[48,384]{1,0:T(8,128)(2,1)S(1)}, bf16[48,384]{1,0:T(8,128)(2,1)S(1)}, u32[]{:S(2)}, u32[]{:S(2)}) collective-permute-start(bf16[48,384]{1,0:T(8,128)(2,1)S(1)} %constant_dynamic-update-slice_fusion.2.refs_0_), channel_id=1, source_target_pairs={{0,6},{1,7},{2,0},{3,1},{4,2},{5,3},{6,4},{7,5},{8,14},{9,15},{10,... | collective-permute-start | bytes 110600 | tf_op jit(solution)/shard_map/ppermute | solution.py:48
  99.2 4.3 %collective-permute-start.20 = (bf16[48,384]{1,0:T(8,128)(2,1)S(1)}, bf16[48,384]{1,0:T(8,128)(2,1)S(1)}, u32[]{:S(2)}, u32[]{:S(2)}) collective-permute-start(bf16[48,384]{1,0:T(8,128)(2,1)S(1)} %constant_dynamic-update-slice_fusion.2.refs_0_), channel_id=1, source_target_pairs={{0,4},{1,5},{2,6},{3,7},{4,0},{5,1},{6,2},{7,3},{8,12},{9,13},{10,... | collective-permute-start | bytes 110600 | tf_op jit(solution)/shard_map/ppermute | solution.py:48
  100.1 4.0 %collective-permute-start.19 = (bf16[48,384]{1,0:T(8,128)(2,1)S(1)}, bf16[48,384]{1,0:T(8,128)(2,1)S(1)}, u32[]{:S(2)}, u32[]{:S(2)}) collective-permute-start(bf16[48,384]{1,0:T(8,128)(2,1)S(1)} %constant_dynamic-update-slice_fusion.2.refs_0_), channel_id=1, source_target_pairs={{0,2},{1,3},{2,4},{3,5},{4,6},{5,7},{6,0},{7,1},{8,10},{9,11},{10,... | collective-permute-start | bytes 110600 | tf_op jit(solution)/shard_map/ppermute | solution.py:48
  104.2 33.3 %all-to-all-start = ((s16[128,40,128]{2,1,0:T(8,128)(2,1)}), s16[128,40,128]{2,1,0:T(8,128)(2,1)}, u32[]{:S(2)}, u32[]{:S(2)}) async-start(s16[128,40,128]{2,1,0:T(8,128)(2,1)} %bitcast.15), calls=%async_computation | async-start | bytes 2621440 | tf_op jit(solution)/shard_map/all_to_all | solution.py:473
  115.5 16.2 %collective-permute-start.27 = (bf16[1,2,48,384]{3,2,1,0:T(8,128)(2,1)S(1)}, bf16[1,2,48,384]{3,2,1,0:T(8,128)(2,1)S(1)}, u32[]{:S(2)}, u32[]{:S(2)}) collective-permute-start(bf16[1,2,48,384]{3,2,1,0:T(8,128)(2,1)S(1)} %bitcast.28), channel_id=1, source_target_pairs={{0,48},{1,49},{2,50},{3,51},{4,52},{5,53},{6,54},{7,55},{8,56},{9,... | collective-permute-start | bytes 221192 | tf_op jit(solution)/shard_map/ppermute | solution.py:48
  118.8 15.3 %collective-permute-start.26 = (bf16[1,2,48,384]{3,2,1,0:T(8,128)(2,1)S(1)}, bf16[1,2,48,384]{3,2,1,0:T(8,128)(2,1)S(1)}, u32[]{:S(2)}, u32[]{:S(2)}) collective-permute-start(bf16[1,2,48,384]{3,2,1,0:T(8,128)(2,1)S(1)} %bitcast.29), channel_id=1, source_target_pairs={{0,32},{1,33},{2,34},{3,35},{4,36},{5,37},{6,38},{7,39},{8,40},{9,... | collective-permute-start | bytes 221192 | tf_op jit(solution)/shard_map/ppermute | solution.py:48
  119.0 17.6 %collective-permute-start.25 = (bf16[1,2,48,384]{3,2,1,0:T(8,128)(2,1)S(1)}, bf16[1,2,48,384]{3,2,1,0:T(8,128)(2,1)S(1)}, u32[]{:S(2)}, u32[]{:S(2)}) collective-permute-start(bf16[1,2,48,384]{3,2,1,0:T(8,128)(2,1)S(1)} %bitcast.30), channel_id=1, source_target_pairs={{0,16},{1,17},{2,18},{3,19},{4,20},{5,21},{6,22},{7,23},{8,24},{9,... | collective-permute-start | bytes 221192 | tf_op jit(solution)/shard_map/ppermute | solution.py:48
  119.7 16.9 %collective-permute-start.24 = (bf16[1,2,48,384]{3,2,1,0:T(8,128)(2,1)S(1)}, bf16[1,2,48,384]{3,2,1,0:T(8,128)(2,1)S(1)}, u32[]{:S(2)}, u32[]{:S(2)}) collective-permute-start(bf16[1,2,48,384]{3,2,1,0:T(8,128)(2,1)S(1)} %bitcast.20), channel_id=1, source_target_pairs={{0,72},{1,73},{2,74},{3,75},{4,76},{5,77},{6,78},{7,79},{8,64},{9,... | collective-permute-start | bytes 221192 | tf_op jit(solution)/shard_map/ppermute | solution.py:48
  122.4 14.3 %collective-permute-start.23 = (bf16[1,2,48,384]{3,2,1,0:T(8,128)(2,1)S(1)}, bf16[1,2,48,384]{3,2,1,0:T(8,128)(2,1)S(1)}, u32[]{:S(2)}, u32[]{:S(2)}) collective-permute-start(bf16[1,2,48,384]{3,2,1,0:T(8,128)(2,1)S(1)} %bitcast.21), channel_id=1, source_target_pairs={{0,8},{1,9},{2,10},{3,11},{4,12},{5,13},{6,14},{7,15},{8,0},{9,1},... | collective-permute-start | bytes 221192 | tf_op jit(solution)/shard_map/ppermute | solution.py:48
  131.7 5.0 %collective-permute-start.22 = (bf16[1,2,48,384]{3,2,1,0:T(8,128)(2,1)S(1)}, bf16[1,2,48,384]{3,2,1,0:T(8,128)(2,1)S(1)}, u32[]{:S(2)}, u32[]{:S(2)}) collective-permute-start(bf16[1,2,48,384]{3,2,1,0:T(8,128)(2,1)S(1)} %bitcast.22), channel_id=1, source_target_pairs={{0,64},{1,65},{2,66},{3,67},{4,68},{5,69},{6,70},{7,71},{8,72},{9,... | collective-permute-start | bytes 221192 | tf_op jit(solution)/shard_map/ppermute | solution.py:48
  137.4 16.4 %collective-permute-start.30 = (bf16[4,2,48,384]{3,2,1,0:T(8,128)(2,1)}, bf16[4,2,48,384]{3,2,1,0:T(8,128)(2,1)S(1)}, u32[]{:S(2)}, u32[]{:S(2)}) collective-permute-start(bf16[4,2,48,384]{3,2,1,0:T(8,128)(2,1)} %pad_maximum_fusion.6), channel_id=1, source_target_pairs={{0,48},{1,49},{2,50},{3,51},{4,52},{5,53},{6,54},{7,55},{8,56},{9,... | collective-permute-start | bytes 884744 | tf_op jit(solution)/shard_map/ppermute | solution.py:48
  141.7 20.4 %collective-permute-start.29 = (bf16[4,2,48,384]{3,2,1,0:T(8,128)(2,1)}, bf16[4,2,48,384]{3,2,1,0:T(8,128)(2,1)S(1)}, u32[]{:S(2)}, u32[]{:S(2)}) collective-permute-start(bf16[4,2,48,384]{3,2,1,0:T(8,128)(2,1)} %pad_maximum_fusion.6), channel_id=1, source_target_pairs={{0,32},{1,33},{2,34},{3,35},{4,36},{5,37},{6,38},{7,39},{8,40},{9,... | collective-permute-start | bytes 884744 | tf_op jit(solution)/shard_map/ppermute | solution.py:48
  141.7 20.4 %collective-permute-start.28 = (bf16[4,2,48,384]{3,2,1,0:T(8,128)(2,1)}, bf16[4,2,48,384]{3,2,1,0:T(8,128)(2,1)S(1)}, u32[]{:S(2)}, u32[]{:S(2)}) collective-permute-start(bf16[4,2,48,384]{3,2,1,0:T(8,128)(2,1)} %pad_maximum_fusion.6), channel_id=1, source_target_pairs={{0,16},{1,17},{2,18},{3,19},{4,20},{5,21},{6,22},{7,23},{8,24},{9,... | collective-permute-start | bytes 884744 | tf_op jit(solution)/shard_map/ppermute | solution.py:48
  142.3 20.0 %collective-permute-start.33 = (bf16[4,2,48,384]{3,2,1,0:T(8,128)(2,1)S(1)}, bf16[4,2,48,384]{3,2,1,0:T(8,128)(2,1)S(1)}, u32[]{:S(2)}, u32[]{:S(2)}) collective-permute-start(bf16[4,2,48,384]{3,2,1,0:T(8,128)(2,1)S(1)} %pad_maximum_fusion.7), channel_id=1, source_target_pairs={{0,72},{1,73},{2,74},{3,75},{4,76},{5,77},{6,78},{7,79},{8,64},{9,... | collective-permute-start | bytes 884744 | tf_op jit(solution)/shard_map/ppermute | solution.py:48
  142.4 19.9 %collective-permute-start.32 = (bf16[4,2,48,384]{3,2,1,0:T(8,128)(2,1)S(1)}, bf16[4,2,48,384]{3,2,1,0:T(8,128)(2,1)S(1)}, u32[]{:S(2)}, u32[]{:S(2)}) collective-permute-start(bf16[4,2,48,384]{3,2,1,0:T(8,128)(2,1)S(1)} %pad_maximum_fusion.7), channel_id=1, source_target_pairs={{0,8},{1,9},{2,10},{3,11},{4,12},{5,13},{6,14},{7,15},{8,0},{9,1},... | collective-permute-start | bytes 884744 | tf_op jit(solution)/shard_map/ppermute | solution.py:48
  144.9 17.1 %copy-start.16 = (bf16[4,2,48,384]{3,2,1,0:T(8,128)(2,1)S(1)}, bf16[4,2,48,384]{3,2,1,0:T(8,128)(2,1)}, u32[]{:S(2)}) copy-start(bf16[4,2,48,384]{3,2,1,0:T(8,128)(2,1)} %pad_maximum_fusion.6) | copy-start | bytes 884740
  153.8 8.5 %collective-permute-start.31 = (bf16[4,2,48,384]{3,2,1,0:T(8,128)(2,1)S(1)}, bf16[4,2,48,384]{3,2,1,0:T(8,128)(2,1)S(1)}, u32[]{:S(2)}, u32[]{:S(2)}) collective-permute-start(bf16[4,2,48,384]{3,2,1,0:T(8,128)(2,1)S(1)} %pad_maximum_fusion.7), channel_id=1, source_target_pairs={{0,64},{1,65},{2,66},{3,67},{4,68},{5,69},{6,70},{7,71},{8,72},{9,... | collective-permute-start | bytes 884744 | tf_op jit(solution)/shard_map/ppermute | solution.py:48
  162.5 4.7 %collective-permute-start.34 = (bf16[16,2,48,384]{3,2,1,0:T(8,128)(2,1)S(1)}, bf16[16,2,48,384]{3,2,1,0:T(8,128)(2,1)S(1)}, u32[]{:S(2)}, u32[]{:S(2)}) collective-permute-start(bf16[16,2,48,384]{3,2,1,0:T(8,128)(2,1)S(1)} %pad_maximum_fusion.2.rest_0_), channel_id=1, source_target_pairs={{0,1},{1,0},{2,3},{3,2},{4,5},{5,4},{6,7},{7,6},{8,9},{9,8},{10,11... | collective-permute-start | bytes 3538952 | tf_op jit(solution)/shard_map/ppermute | solution.py:48
  164.7 4.2 %collective-permute-start.35 = (bf16[16,2,48,384]{3,2,1,0:T(8,128)(2,1)S(1)}, bf16[16,2,48,384]{3,2,1,0:T(8,128)(2,1)S(1)}, u32[]{:S(2)}, u32[]{:S(2)}) collective-permute-start(bf16[16,2,48,384]{3,2,1,0:T(8,128)(2,1)S(1)} %pad_maximum_fusion.3.rest_2_), channel_id=1, source_target_pairs={{0,1},{1,0},{2,3},{3,2},{4,5},{5,4},{6,7},{7,6},{8,9},{9,8},{10,11... | collective-permute-start | bytes 3538952 | tf_op jit(solution)/shard_map/ppermute | solution.py:48
  (7 other events, 31.9 us)

commit v2 on v1

--- a/solution.py
+++ b/solution.py
@@ -39,32 +39,34 @@
     return ((x % 2) * 4 + z) * 16 + (x // 2) * 8 + y * 2 + core
 
 
-def shifted(values, axis, step):
+def shifted(values, axes, step):
     pairs = []
     for source in range(DEVICES):
         place = coords(source)
+        axis = axes[place[3]]
         place[axis] = (place[axis] + step) % (2 if axis == 3 else 4)
         pairs.append((source, device_at(*place)))
     return lax.ppermute(values, AXES, pairs)
 
 
-def ring(block, axis):
+def ring(block, axes):
     return jnp.concatenate(
-        [block, shifted(block, axis, 1), shifted(block, axis, 2), shifted(block, axis, -1)], 0
+        [block, shifted(block, axes, 1), shifted(block, axes, 2), shifted(block, axes, -1)], 0
     )
 
 
 def merge_kernel(scalar_ref, *refs):
     to = lax.broadcasted_iota(jnp.int32, (192, 192), 0)
     of = lax.broadcasted_iota(jnp.int32, (192, 192), 1)
-    head, y, core, row = to // 48, (to // 12) % 4, (to // 6) % 2, to % 6
+    head, half, y, core, row = to // 96, (to // 48) % 2, (to // 12) % 4, (to // 6) % 2, to % 6
     behind = (scalar_ref[1] - y) & 3
-    source = (behind * 2 + (core ^ scalar_ref[3])) * 24 + row * 4 + head
+    source = (behind * 2 + (core ^ scalar_ref[3])) * 24 + half * 12 + row * 2 + head
     order = jnp.where(of == source, 1.0, 0.0).astype(BF16)
     slots = jnp.concatenate([ref[...] for ref in refs[:4]], axis=0)
     ordered = dot(order, slots).astype(BF16)
-    for head_at in range(HEADS):
-        refs[4 + head_at // 2][head_at % 2] = ordered[head_at * 48 : (head_at + 1) * 48]
+    for part in range(4):
+        lanes = slice(part % 2 * 384, (part % 2 + 1) * 384)
+        refs[4][0, part // 2, :, lanes] = ordered[part * 48 : (part + 1) * 48]
 
 
 def merge(scalars, slots):
@@ -72,26 +74,23 @@
     return pl.pallas_call(
         merge_kernel,
         in_specs=[pl.BlockSpec(memory_space=pltpu.SMEM)] + [vmem] * 4,
-        out_shape=[jax.ShapeDtypeStruct((2, 48, 384), BF16)] * 2,
+        out_shape=jax.ShapeDtypeStruct((1, 2, 48, TOKENS), BF16),
         compiler_params=pltpu.CompilerParams(vmem_limit_bytes=8 * MIB),
         cost_estimate=pl.CostEstimate(flops=10**7, bytes_accessed=3 * 10**5, transcendentals=0),
     )(scalars, *slots)
 
 
 def gather_plane(place, kept, sent, beside, work, crossing=False):
-    block = jnp.concatenate([kept, shifted(sent, 3, 1)], axis=0)
-    slots = [block] + [shifted(block, 1, step) for step in (1, 2, -1)]
+    block = jnp.concatenate([kept, shifted(sent, (3, 3), 1)], axis=0)
+    slots = [block] + [shifted(block, (1, 1), step) for step in (1, 2, -1)]
     if crossing:
         *slots, beside = lax.optimization_barrier((*slots, beside))
         beside = cross(beside)
-    blocks = [ring(pair[None], axis) for pair, axis in zip(merge(place, slots), (0, 2))]
-    blocks, beside = lax.optimization_barrier((blocks, beside))
-    blocks = [ring(block, axis) for block, axis in zip(blocks, (2, 0))]
-    blocks, done = lax.optimization_barrier((blocks, work(beside)))
-    pieces = []
-    for block in blocks:
-        pieces += [block, shifted(block, 3, 1)]
-    return pieces, done
+    block = ring(merge(place, slots), (0, 2))
+    block, beside = lax.optimization_barrier((block, beside))
+    block = ring(block, (2, 0))
+    block, done = lax.optimization_barrier((block, work(beside)))
+    return [block, shifted(block, (3, 3), 1)], done
 
 
 def split(values):
@@ -148,9 +147,11 @@
 
         @pl.when(step == row)
         def _():
-            for half in range(2):
-                at = half * 24 + row * 4
-                rows_ref[at : at + 4, :] = bias[:, half * 384 : (half + 1) * 384]
+            for part in range(4):
+                pair, half = part // 2, part % 2
+                at = pair * 24 + half * 12 + row * 2
+                lanes = slice(half * 384, (half + 1) * 384)
+                rows_ref[at : at + 2, :] = bias[pair * 2 : pair * 2 + 2, lanes]
 
 
 def hand_over(scalar_ref, rows_ref, kept_ref, sent_ref):
@@ -299,30 +300,22 @@
         x_hi, z, x_lo = group % 2, (group // 2) % 4, group // 8
         behind_x, behind_z = (my_x - (x_hi * 2 + x_lo)) & 3, (my_z - z) & 3
         rows = pl.ds(pl.multiple_of(group * 48, 16), 48)
-
-        def one_half(own):
-            half = core if own else 1 - core
-            lanes = pl.ds(pl.multiple_of(half * 384, 128), 384)
-            needed = group * 48 < limit if turned else half * 384 < limit
-
-            @pl.when(needed)
-            def _():
-                for head in range(HEADS):
-                    if head < 2:
-                        at = behind_z * 4 + behind_x
-                    else:
-                        at = behind_x * 4 + behind_z
-                    values = piece_refs[head // 2 * 2 + (0 if own else 1)][at, head % 2]
-                    if turned:
-                        flat_ref[head, rows, lanes] = values
-                    else:
-                        key = lax.broadcasted_iota(jnp.int32, (48, 384), 1) + half * 384
-                        plane_ref[head, rows, lanes] = jnp.where(
-                            key < real, values.astype(F32) * LOG2E, NEGATIVE
-                        )
-
-        one_half(True)
-        one_half(False)
+        for ref, pair in zip(piece_refs, (core, 1 - core)):
+            at = jnp.where(pair == 0, behind_z * 4 + behind_x, behind_x * 4 + behind_z)
+            for half in range(2):
+                lanes = slice(half * 384, (half + 1) * 384)
+
+                @pl.when(group * 48 < limit if turned else half * 384 < limit)
+                def _():
+                    for odd in range(2):
+                        values = ref[at, odd, :, lanes]
+                        if turned:
+                            flat_ref[pair * 2 + odd, rows, lanes] = values
+                        else:
+                            key = lax.broadcasted_iota(jnp.int32, (48, 384), 1) + half * 384
+                            plane_ref[pair * 2 + odd, rows, lanes] = jnp.where(
+                                key < real, values.astype(F32) * LOG2E, NEGATIVE
+                            )
         return 0
 
     lax.fori_loop(0, 16, one_group, 0)
@@ -361,7 +354,7 @@
 
 
 def attend_kernel(turned, scalar_ref, q_ref, k_ref, v_ref, g_ref, wo_ref, *rest):
-    piece_refs, rest = rest[:4], rest[4:]
+    piece_refs, rest = rest[:2], rest[2:]
     step = pl.program_id(0)
     if turned:
         crossed_ref, plane_ref, mixed_ref, flat_ref = rest
@@ -414,7 +407,7 @@
     head_spec = pl.BlockSpec((1, HEADS, TOKENS, HD), lambda i: (i, 0, 0, 0))
     in_specs = [pl.BlockSpec(memory_space=pltpu.SMEM), head_spec, head_spec]
     in_specs += [pl.BlockSpec((1, TOKENS, 2 * HD), lambda i: (i, 0, 0)), row_spec]
-    in_specs += [matrix(turned)] + [whole] * 4
+    in_specs += [matrix(turned)] + [whole] * 2
     out_shape = [jax.ShapeDtypeStruct((DEVICES * PADDED, HD), F32 if turned else jnp.int16)]
     out_specs = [pl.BlockSpec((DEVICES * PADDED, HD), lambda i: (0, 0))]
     scratch = [pltpu.VMEM((HEADS, TOKENS, TOKENS), F32), pltpu.VMEM((TOKENS, HD), F32)]

time: 228 us -> 180 us (0.79); the launches traced: 230 us -> 179 us
  Pallas kernels: 88.3 us -> 56.8 us
  starting transfers between devices: 58.6 us -> 34.5 us
  waiting for transfers between devices: 43 us -> 50.7 us
    pallas_call x2, Pallas kernels: 60.3 us -> 28.6 us  [run_pass(): pl.pallas_call(functools.partial(attend_kernel, turned), grid=(ROWS,), in...]
    ppermute x36 -> x22, starting transfers between devices: 48.1 us -> 28.8 us  [shifted(): return lax.ppermute(values, AXES, pairs)]
    ppermute x36 -> x22, waiting for transfers between devices: 43 us -> 50.7 us  [shifted(): return lax.ppermute(values, AXES, pairs)]
    all_to_all x1, starting transfers between devices: 10.5 us -> 5.74 us  [cross(): return lax.all_to_all(values, AXES, split_axis=0, concat_axis=0, tiled=True)]
  transfers between devices with their start and end apart: 37 -> 23, of which waited for: 19 -> 19; matrix products, arithmetic and copies ran while one was open for 2% -> 2% of each run, Pallas kernels for 8% -> 11%
where the time goes in v2:
time: 180 us; the launch traced here: 179 us
  Pallas kernels  56.8 us (32%)
  waiting for transfers between devices  50.7 us (28%)
  starting transfers between devices  34.5 us (19%)
  blocking collectives  27.4 us (15%)
  local copies, waits for them, and re-layouts  5.47 us (3%)
  other arithmetic  4.33 us (2%)
    ppermute x22, waiting for transfers between devices, shifted(): return lax.ppermute(values, AXES, pairs)  50.7 us
    ppermute x22, starting transfers between devices, shifted(): return lax.ppermute(values, AXES, pairs)  28.8 us
    pallas_call x2, Pallas kernels, run_pass(): pl.pallas_call(functools.partial(attend_kernel, turned), grid=(ROWS,), in...  28.6 us
    all_to_all x1, blocking collectives, cross(): return lax.all_to_all(values, AXES, split_axis=0, concat_axis=0, tiled=True)  27.4 us
    pallas_call x2, Pallas kernels, project(): pl.pallas_call(functools.partial(project_kernel, crossed), grid=(ROWS,),...  18.5 us
    all_to_all x1, starting transfers between devices, cross(): return lax.all_to_all(values, AXES, split_axis=0, concat_axis=0, tiled=True)  5.74 us
    pallas_call x1, Pallas kernels, first_bias(): pl.pallas_call(bias_kernel, grid=(ROWS,), in_specs=[pl.BlockSpec(memory_s...  5.24 us
    unnamed x38, local copies, waits for them, and re-layouts  4.82 us
  transfers between devices with their start and end apart: 23, of which 19 were waited for; matrix products, arithmetic and copies ran while one was open for 2% of the time, Pallas kernels for 11%

profile of v2, /device:TPU:1, one launch (start us, length us, event | category | flops | bytes accessed | tf_op | source)
XLA Modules:
  0.0 179.5 jit_solution(16144328761075262713)
XLA Ops:
  0.2 1.7 copy-done
  1.8 0.7 copy-done.4
  2.5 0.7 copy-done.6
  3.2 0.7 copy-done.8
  3.9 5.2 %shard_map.109 = (bf16[24,384]{1,0:T(8,128)(2,1)S(1)}, bf16[24,384]{1,0:T(8,128)(2,1)S(1)}) custom-call(s32[4]{0:T(128)S(1)} %pad_add_fusion.scalar_ref, f32[6,768,128]{2,1,0:T(8,128)S(1)} %copy-done, f32[2,128]{1,0:T(2,128)S(1)} %copy-done.6, f32[2,128]{1,0:T(2,128)S(1)} %copy-done.8, f32[2,4,128]{2,1,0:T(4,128)S(1)} %copy-done.4), custom_call_target="tpu_custom_call" | custom-call | flops 100000000 | bytes 2000000 | tf_op jit(solution)/shard_map/pallas_call | solution.py:178
  9.1 1.5 collective-permute-start
  10.6 0.8 collective-permute-done
  11.5 2.8 %collective-permute-start.3 = (bf16[48,384]{1,0:T(8,128)(2,1)S(1)}, bf16[48,384]{1,0:T(8,128)(2,1)S(1)}, u32[]{:S(2)}, u32[]{:S(2)}) collective-permute-start(bf16[48,384]{1,0:T(8,128)(2,1)S(1)} %constant_dynamic-update-slice_fusion.refs_0_), channel_id=1, source_target_pairs={{0,6},{1,7},{2,0},{3,1},{4,2},{5,3},{6,4},{7,5},{8,14},{9,15},{10,... | collective-permute-start | bytes 110600 | tf_op jit(solution)/shard_map/ppermute | solution.py:49
  14.7 0.7 collective-permute-start.1
  15.4 3.3 %collective-permute-done.2.refs_2_ = bf16[48,384]{1,0:T(8,128)(2,1)S(1)} collective-permute-done((bf16[48,384]{1,0:T(8,128)(2,1)S(1)}, bf16[48,384]{1,0:T(8,128)(2,1)S(1)}, u32[]{:S(2)}, u32[]{:S(2)}) %collective-permute-start.2) | collective-permute-done | bytes 36896 | tf_op jit(solution)/shard_map/ppermute | solution.py:49
  19.0 0.9 shard_map.110
  19.9 3.8 %collective-permute-start.6 = (bf16[1,2,48,768]{3,2,1,0:T(8,128)(2,1)S(1)}, bf16[1,2,48,768]{3,2,1,0:T(8,128)(2,1)S(1)}, u32[]{:S(2)}, u32[]{:S(2)}) collective-permute-start(bf16[1,2,48,768]{3,2,1,0:T(8,128)(2,1)S(1)} %shard_map.110), channel_id=1, source_target_pairs={{0,72},{1,49},{2,74},{3,51},{4,76},{5,53},{6,78},{7,55},{8,64},{9,... | collective-permute-start | bytes 442376 | tf_op jit(solution)/shard_map/ppermute | solution.py:49
  23.7 0.7 collective-permute-start.4
  25.0 0.6 concatenate.24.scalar_ref
  25.6 1.7 collective-permute-done.6
  27.4 2.2 %collective-permute-done.5 = bf16[1,2,48,768]{3,2,1,0:T(8,128)(2,1)S(1)} collective-permute-done((bf16[1,2,48,768]{3,2,1,0:T(8,128)(2,1)S(1)}, bf16[1,2,48,768]{3,2,1,0:T(8,128)(2,1)S(1)}, u32[]{:S(2)}, u32[]{:S(2)}) %collective-permute-start.5) | collective-permute-done | bytes 147488 | tf_op jit(solution)/shard_map/ppermute | solution.py:49
  29.5 1.2 collective-permute-done.4
  30.9 2.3 %collective-permute-start.9 = (bf16[4,2,48,768]{3,2,1,0:T(8,128)(2,1)S(1)}, bf16[4,2,48,768]{3,2,1,0:T(8,128)(2,1)S(1)}, u32[]{:S(2)}, u32[]{:S(2)}) collective-permute-start(bf16[4,2,48,768]{3,2,1,0:T(8,128)(2,1)S(1)} %pad_maximum_fusion.2), channel_id=1, source_target_pairs={{0,48},{1,73},{2,50},{3,75},{4,52},{5,77},{6,54},{7,79},{8,56},{9,... | collective-permute-start | bytes 1769480 | tf_op jit(solution)/shard_map/ppermute | solution.py:49
  34.3 10.3 %shard_map.111 = (bf16[6,4,768,128]{3,2,1,0:T(8,128)(2,1)S(1)}, bf16[6,4,768,128]{3,2,1,0:T(8,128)(2,1)S(1)}, bf16[6,768,256]{2,1,0:T(8,128)(2,1)S(1)}, f32[6,768,128]{2,1,0:T(8,128)S(1)}) custom-call(f32[6,768,128]{2,1,0:T(8,128)S(1)} %copy-done.1, f32[2,128]{1,0:T(2,128)S(1)} %copy-done.7, f32[2,128]{1,0:T(2,128)S(1)} %copy-done.9, ...), custom_call_target="tpu_custom_call" | custom-call | flops 10000000000 | bytes 17000000 | tf_op jit(solution)/shard_map/pallas_call | solution.py:272
  44.6 1.7 collective-permute-done.9
  46.3 3.7 %collective-permute-done.7 = bf16[4,2,48,768]{3,2,1,0:T(8,128)(2,1)S(1)} collective-permute-done((bf16[4,2,48,768]{3,2,1,0:T(8,128)(2,1)S(1)}, bf16[4,2,48,768]{3,2,1,0:T(8,128)(2,1)S(1)}, u32[]{:S(2)}, u32[]{:S(2)}) %collective-permute-start.7) | collective-permute-done | bytes 589856 | tf_op jit(solution)/shard_map/ppermute | solution.py:49
  50.3 4.6 %collective-permute-start.10 = (bf16[16,2,48,768]{3,2,1,0:T(8,128)(2,1)S(1)}, bf16[16,2,48,768]{3,2,1,0:T(8,128)(2,1)S(1)}, u32[]{:S(2)}, u32[]{:S(2)}) collective-permute-start(bf16[16,2,48,768]{3,2,1,0:T(8,128)(2,1)S(1)} %pad_maximum_fusion.rest_0_), channel_id=1, source_target_pairs={{0,1},{1,0},{2,3},{3,2},{4,5},{5,4},{6,7},{7,6},{8,9},{9,8},{10,11... | collective-permute-start | bytes 7077896 | tf_op jit(solution)/shard_map/ppermute | solution.py:49
  54.9 4.2 %collective-permute-done.10.rest_1_ = bf16[16,2,48,768]{3,2,1,0:T(8,128)(2,1)S(1)} collective-permute-done((bf16[16,2,48,768]{3,2,1,0:T(8,128)(2,1)S(1)}, bf16[16,2,48,768]{3,2,1,0:T(8,128)(2,1)S(1)}, u32[]{:S(2)}, u32[]{:S(2)}) %collective-permute-start.10) | collective-permute-done | bytes 2359328 | tf_op jit(solution)/shard_map/ppermute | solution.py:49
  59.0 16.8 %shard_map.112 = (f32[6,768,128]{2,1,0:T(8,128)S(1)}, s16[5120,128]{1,0:T(8,128)(2,1)S(1)}, bf16[24,384]{1,0:T(8,128)(2,1)S(1)}, bf16[24,384]{1,0:T(8,128)(2,1)S(1)}) custom-call(s32[5]{0:T(128)S(1)} %concatenate.24.scalar_ref, bf16[6,4,768,128]{3,2,1,0:T(8,128)(2,1)S(1)} %get-tuple-element.50.q_ref, bf16[6,4,768,128]{3,2,1,0:T(8,128)(2,1)S(1)} %get-tuple-element.51.k_ref, ...), custom_call_target="tpu_custom_call" | custom-call | flops 20000000000 | bytes 20000000 | tf_op jit(solution)/shard_map/pallas_call | solution.py:424
  75.8 1.0 copy-done.3
  77.3 0.8 collective-permute-done.11
  78.4 1.1 collective-permute-start.13
  79.5 0.8 collective-permute-start.12
  80.9 1.8 collective-permute-done.13.refs_2_
  82.7 1.4 collective-permute-done.12.refs_1_
  84.1 5.7 %all-to-all-start = ((s16[128,40,128]{2,1,0:T(8,128)(2,1)}), s16[128,40,128]{2,1,0:T(8,128)(2,1)}, u32[]{:S(2)}, u32[]{:S(2)}) async-start(s16[128,40,128]{2,1,0:T(8,128)(2,1)} %bitcast.11), calls=%async_computation | async-start | bytes 2621440 | tf_op jit(solution)/shard_map/all_to_all | solution.py:466
  89.8 0.9 shard_map.113
  90.7 3.4 %collective-permute-start.17 = (bf16[1,2,48,768]{3,2,1,0:T(8,128)(2,1)S(1)}, bf16[1,2,48,768]{3,2,1,0:T(8,128)(2,1)S(1)}, u32[]{:S(2)}, u32[]{:S(2)}) collective-permute-start(bf16[1,2,48,768]{3,2,1,0:T(8,128)(2,1)S(1)} %shard_map.113), channel_id=1, source_target_pairs={{0,72},{1,49},{2,74},{3,51},{4,76},{5,53},{6,78},{7,55},{8,64},{9,... | collective-permute-start | bytes 442376 | tf_op jit(solution)/shard_map/ppermute | solution.py:49
  94.3 0.8 collective-permute-start.15
  95.0 13.0 %collective-permute-done.17 = bf16[1,2,48,768]{3,2,1,0:T(8,128)(2,1)S(1)} collective-permute-done((bf16[1,2,48,768]{3,2,1,0:T(8,128)(2,1)S(1)}, bf16[1,2,48,768]{3,2,1,0:T(8,128)(2,1)S(1)}, u32[]{:S(2)}, u32[]{:S(2)}) %collective-permute-start.17) | collective-permute-done | bytes 147488 | tf_op jit(solution)/shard_map/ppermute | solution.py:49
  108.0 1.6 collective-permute-done.16
  109.6 2.4 %collective-permute-done.15 = bf16[1,2,48,768]{3,2,1,0:T(8,128)(2,1)S(1)} collective-permute-done((bf16[1,2,48,768]{3,2,1,0:T(8,128)(2,1)S(1)}, bf16[1,2,48,768]{3,2,1,0:T(8,128)(2,1)S(1)}, u32[]{:S(2)}, u32[]{:S(2)}) %collective-permute-start.15) | collective-permute-done | bytes 147488 | tf_op jit(solution)/shard_map/ppermute | solution.py:49
  112.0 0.9 pad_maximum_fusion.3
  112.9 2.2 %collective-permute-start.20 = (bf16[4,2,48,768]{3,2,1,0:T(8,128)(2,1)}, bf16[4,2,48,768]{3,2,1,0:T(8,128)(2,1)S(1)}, u32[]{:S(2)}, u32[]{:S(2)}) collective-permute-start(bf16[4,2,48,768]{3,2,1,0:T(8,128)(2,1)} %pad_maximum_fusion.3), channel_id=1, source_target_pairs={{0,48},{1,73},{2,50},{3,75},{4,52},{5,77},{6,54},{7,79},{8,56},{9,... | collective-permute-start | bytes 1769480 | tf_op jit(solution)/shard_map/ppermute | solution.py:49
  115.6 0.9 collective-permute-start.18
  116.4 1.7 convert_element_type.11.x_ref
  118.1 8.2 %shard_map.114 = (bf16[6,4,768,128]{3,2,1,0:T(8,128)(2,1)S(1)}, bf16[6,4,768,128]{3,2,1,0:T(8,128)(2,1)S(1)}, bf16[6,768,256]{2,1,0:T(8,128)(2,1)S(1)}, f32[6,768,128]{2,1,0:T(8,128)S(1)}) custom-call(f32[5120,128]{1,0:T(8,128)S(1)} %convert_element_type.11.x_ref, f32[2,128]{1,0:T(2,128)S(1)} %copy-done.7, f32[2,128]{1,0:T(2,128)S(1)} %copy-done.9, ...), custom_call_target="tpu_custom_call" | custom-call | flops 10000000000 | bytes 17000000 | tf_op jit(solution)/shard_map/pallas_call | solution.py:272
  126.3 2.3 %collective-permute-done.20 = bf16[4,2,48,768]{3,2,1,0:T(8,128)(2,1)S(1)} collective-permute-done((bf16[4,2,48,768]{3,2,1,0:T(8,128)(2,1)}, bf16[4,2,48,768]{3,2,1,0:T(8,128)(2,1)S(1)}, u32[]{:S(2)}, u32[]{:S(2)}) %collective-permute-start.20) | collective-permute-done | bytes 589856 | tf_op jit(solution)/shard_map/ppermute | solution.py:49
  128.6 3.5 %collective-permute-done.18 = bf16[4,2,48,768]{3,2,1,0:T(8,128)(2,1)S(1)} collective-permute-done((bf16[4,2,48,768]{3,2,1,0:T(8,128)(2,1)}, bf16[4,2,48,768]{3,2,1,0:T(8,128)(2,1)S(1)}, u32[]{:S(2)}, u32[]{:S(2)}) %collective-permute-start.18) | collective-permute-done | bytes 589856 | tf_op jit(solution)/shard_map/ppermute | solution.py:49
  132.9 4.2 %collective-permute-done.21.rest_1_ = bf16[16,2,48,768]{3,2,1,0:T(8,128)(2,1)S(1)} collective-permute-done((bf16[16,2,48,768]{3,2,1,0:T(8,128)(2,1)S(1)}, bf16[16,2,48,768]{3,2,1,0:T(8,128)(2,1)S(1)}, u32[]{:S(2)}, u32[]{:S(2)}) %collective-permute-start.21) | collective-permute-done | bytes 2359328 | tf_op jit(solution)/shard_map/ppermute | solution.py:49
  137.1 11.8 %shard_map.115 = f32[5120,128]{1,0:T(8,128)S(1)} custom-call(s32[5]{0:T(128)S(1)} %concatenate.24.scalar_ref, bf16[6,4,768,128]{3,2,1,0:T(8,128)(2,1)S(1)} %get-tuple-element.70.q_ref, bf16[6,4,768,128]{3,2,1,0:T(8,128)(2,1)S(1)} %get-tuple-element.71.k_ref, bf16[6,768,256]{2,1,0:T(8,128)(2,1)S(1)} %get-tuple-element.72.v_ref, ...), custom_call_target="tpu_custom_call" | custom-call | flops 20000000000 | bytes 20000000 | tf_op jit(solution)/shard_map/pallas_call | solution.py:424
  149.1 27.4 %all_to_all.21 = f16[128,40,128]{2,1,0:T(8,128)(2,1)S(1)} all-to-all(f16[128,40,128]{2,1,0:T(8,128)(2,1)S(1)} %bitcast.12), channel_id=1, replica_groups=mesh['row'=8,'col'=16] {'row','col'}, dimensions={0} | all-to-all | bytes 2621440 | tf_op jit(solution)/shard_map/all_to_all | solution.py:466
  176.7 2.8 %shard_map.116 = f32[6,768,128]{2,1,0:T(8,128)} custom-call(f32[6,768,128]{2,1,0:T(8,128)S(1)} %get-tuple-element.55.first_ref, f32[5120,128]{1,0:T(8,128)S(1)} %bitcast_convert_fusion.update_ref), custom_call_target="tpu_custom_call" | custom-call | flops 1000000 | bytes 8000000 | tf_op jit(solution)/shard_map/pallas_call | solution.py:451
  (57 shorter events, 6.1 us)
Async XLA Ops:
  0.0 34.2 %copy-start.9 = (f32[2,128]{1,0:T(2,128)S(1)}, f32[2,128]{1,0:T(2,128)}, u32[]{:S(2)}) copy-start(f32[2,128]{1,0:T(2,128)} %shift_ref.5) | copy-start | bytes 3076
  0.0 34.2 %copy-start.7 = (f32[2,128]{1,0:T(2,128)S(1)}, f32[2,128]{1,0:T(2,128)}, u32[]{:S(2)}) copy-start(f32[2,128]{1,0:T(2,128)} %gain_ref.5) | copy-start | bytes 3076
  0.0 24.4 %copy-start.17 = (s32[768]{0:T(1024)S(1)}, s32[768]{0:T(1024)}, u32[]{:S(2)}) copy-start(s32[768]{0:T(1024)} %param.12) | copy-start | bytes 9220
  0.0 34.2 %copy-start.15 = (f32[2,128]{1,0:T(2,128)S(1)}, f32[2,128]{1,0:T(2,128)}, u32[]{:S(2)}) copy-start(f32[2,128]{1,0:T(2,128)} %gs_ref.3) | copy-start | bytes 3076
  0.0 34.2 %copy-start.10 = (f32[2,128,128]{2,1,0:T(8,128)S(1)}, f32[2,128,128]{2,1,0:T(8,128)}, u32[]{:S(2)}) copy-start(f32[2,128,128]{2,1,0:T(8,128)} %wq_ref.3) | copy-start | bytes 393220
  0.2 1.7 copy-start
  1.8 0.7 copy-start.4
  2.5 0.7 copy-start.6
  3.2 0.7 copy-start.8
  3.9 30.4 %copy-start.1 = (f32[6,768,128]{2,1,0:T(8,128)S(1)}, f32[6,768,128]{2,1,0:T(8,128)}, u32[]{:S(2)}) copy-start(f32[6,768,128]{2,1,0:T(8,128)} %rest_2_.1) | copy-start | bytes 7077892
  3.9 30.4 %copy-start.11 = (f32[2,128,128]{2,1,0:T(8,128)S(1)}, f32[2,128,128]{2,1,0:T(8,128)}, u32[]{:S(2)}) copy-start(f32[2,128,128]{2,1,0:T(8,128)} %wk_ref.3) | copy-start | bytes 393220
  3.9 30.4 %copy-start.12 = (f32[2,128,128]{2,1,0:T(8,128)S(1)}, f32[2,128,128]{2,1,0:T(8,128)}, u32[]{:S(2)}) copy-start(f32[2,128,128]{2,1,0:T(8,128)} %wv_ref.3) | copy-start | bytes 393220
  3.9 30.4 %copy-start.13 = (f32[2,128,128]{2,1,0:T(8,128)S(1)}, f32[2,128,128]{2,1,0:T(8,128)}, u32[]{:S(2)}) copy-start(f32[2,128,128]{2,1,0:T(8,128)} %wg_ref.3) | copy-start | bytes 393220
  9.1 2.3 %collective-permute-start = (bf16[24,384]{1,0:T(8,128)(2,1)S(1)}, bf16[24,384]{1,0:T(8,128)(2,1)S(1)}, u32[]{:S(2)}, u32[]{:S(2)}) collective-permute-start(bf16[24,384]{1,0:T(8,128)(2,1)S(1)} %get-tuple-element.41), channel_id=1, source_target_pairs={{0,1},{1,0},{2,3},{3,2},{4,5},{5,4},{6,7},{7,6},{8,9},{9,8},{10,11... | collective-permute-start | bytes 55304 | tf_op jit(solution)/shard_map/ppermute | solution.py:49
  11.5 3.9 %collective-permute-start.3 = (bf16[48,384]{1,0:T(8,128)(2,1)S(1)}, bf16[48,384]{1,0:T(8,128)(2,1)S(1)}, u32[]{:S(2)}, u32[]{:S(2)}) collective-permute-start(bf16[48,384]{1,0:T(8,128)(2,1)S(1)} %constant_dynamic-update-slice_fusion.refs_0_), channel_id=1, source_target_pairs={{0,6},{1,7},{2,0},{3,1},{4,2},{5,3},{6,4},{7,5},{8,14},{9,15},{10,... | collective-permute-start | bytes 110600 | tf_op jit(solution)/shard_map/ppermute | solution.py:49
  14.3 4.3 %collective-permute-start.2 = (bf16[48,384]{1,0:T(8,128)(2,1)S(1)}, bf16[48,384]{1,0:T(8,128)(2,1)S(1)}, u32[]{:S(2)}, u32[]{:S(2)}) collective-permute-start(bf16[48,384]{1,0:T(8,128)(2,1)S(1)} %constant_dynamic-update-slice_fusion.refs_0_), channel_id=1, source_target_pairs={{0,4},{1,5},{2,6},{3,7},{4,0},{5,1},{6,2},{7,3},{8,12},{9,13},{10,... | collective-permute-start | bytes 110600 | tf_op jit(solution)/shard_map/ppermute | solution.py:49
  14.7 4.4 %collective-permute-start.1 = (bf16[48,384]{1,0:T(8,128)(2,1)S(1)}, bf16[48,384]{1,0:T(8,128)(2,1)S(1)}, u32[]{:S(2)}, u32[]{:S(2)}) collective-permute-start(bf16[48,384]{1,0:T(8,128)(2,1)S(1)} %constant_dynamic-update-slice_fusion.refs_0_), channel_id=1, source_target_pairs={{0,2},{1,3},{2,4},{3,5},{4,6},{5,7},{6,0},{7,1},{8,10},{9,11},{10,... | collective-permute-start | bytes 110600 | tf_op jit(solution)/shard_map/ppermute | solution.py:49
  19.9 7.5 %collective-permute-start.6 = (bf16[1,2,48,768]{3,2,1,0:T(8,128)(2,1)S(1)}, bf16[1,2,48,768]{3,2,1,0:T(8,128)(2,1)S(1)}, u32[]{:S(2)}, u32[]{:S(2)}) collective-permute-start(bf16[1,2,48,768]{3,2,1,0:T(8,128)(2,1)S(1)} %shard_map.110), channel_id=1, source_target_pairs={{0,72},{1,49},{2,74},{3,51},{4,76},{5,53},{6,78},{7,55},{8,64},{9,... | collective-permute-start | bytes 442376 | tf_op jit(solution)/shard_map/ppermute | solution.py:49
  23.7 5.8 %collective-permute-start.5 = (bf16[1,2,48,768]{3,2,1,0:T(8,128)(2,1)S(1)}, bf16[1,2,48,768]{3,2,1,0:T(8,128)(2,1)S(1)}, u32[]{:S(2)}, u32[]{:S(2)}) collective-permute-start(bf16[1,2,48,768]{3,2,1,0:T(8,128)(2,1)S(1)} %shard_map.110), channel_id=1, source_target_pairs={{0,8},{1,33},{2,10},{3,35},{4,12},{5,37},{6,14},{7,39},{8,0},{9,41... | collective-permute-start | bytes 442376 | tf_op jit(solution)/shard_map/ppermute | solution.py:49
  23.7 7.1 %collective-permute-start.4 = (bf16[1,2,48,768]{3,2,1,0:T(8,128)(2,1)S(1)}, bf16[1,2,48,768]{3,2,1,0:T(8,128)(2,1)S(1)}, u32[]{:S(2)}, u32[]{:S(2)}) collective-permute-start(bf16[1,2,48,768]{3,2,1,0:T(8,128)(2,1)S(1)} %shard_map.110), channel_id=1, source_target_pairs={{0,64},{1,17},{2,66},{3,19},{4,68},{5,21},{6,70},{7,23},{8,72},{9,... | collective-permute-start | bytes 442376 | tf_op jit(solution)/shard_map/ppermute | solution.py:49
  30.9 15.4 %collective-permute-start.9 = (bf16[4,2,48,768]{3,2,1,0:T(8,128)(2,1)S(1)}, bf16[4,2,48,768]{3,2,1,0:T(8,128)(2,1)S(1)}, u32[]{:S(2)}, u32[]{:S(2)}) collective-permute-start(bf16[4,2,48,768]{3,2,1,0:T(8,128)(2,1)S(1)} %pad_maximum_fusion.2), channel_id=1, source_target_pairs={{0,48},{1,73},{2,50},{3,75},{4,52},{5,77},{6,54},{7,79},{8,56},{9,... | collective-permute-start | bytes 1769480 | tf_op jit(solution)/shard_map/ppermute | solution.py:49
  33.1 13.2 %collective-permute-start.8 = (bf16[4,2,48,768]{3,2,1,0:T(8,128)(2,1)S(1)}, bf16[4,2,48,768]{3,2,1,0:T(8,128)(2,1)S(1)}, u32[]{:S(2)}, u32[]{:S(2)}) collective-permute-start(bf16[4,2,48,768]{3,2,1,0:T(8,128)(2,1)S(1)} %pad_maximum_fusion.2), channel_id=1, source_target_pairs={{0,32},{1,9},{2,34},{3,11},{4,36},{5,13},{6,38},{7,15},{8,40},{9,1... | collective-permute-start | bytes 1769480 | tf_op jit(solution)/shard_map/ppermute | solution.py:49
  33.6 16.3 %collective-permute-start.7 = (bf16[4,2,48,768]{3,2,1,0:T(8,128)(2,1)S(1)}, bf16[4,2,48,768]{3,2,1,0:T(8,128)(2,1)S(1)}, u32[]{:S(2)}, u32[]{:S(2)}) collective-permute-start(bf16[4,2,48,768]{3,2,1,0:T(8,128)(2,1)S(1)} %pad_maximum_fusion.2), channel_id=1, source_target_pairs={{0,16},{1,65},{2,18},{3,67},{4,20},{5,69},{6,22},{7,71},{8,24},{9,... | collective-permute-start | bytes 1769480 | tf_op jit(solution)/shard_map/ppermute | solution.py:49
  44.5 14.5 %copy-start.2 = (f32[6,768,128]{2,1,0:T(8,128)S(1)}, f32[6,768,128]{2,1,0:T(8,128)}, u32[]{:S(2)}) copy-start(f32[6,768,128]{2,1,0:T(8,128)} %rest_2_.1) | copy-start | bytes 7077892
  44.6 14.5 %copy-start.5 = (f32[2,4,128]{2,1,0:T(4,128)S(1)}, f32[2,4,128]{2,1,0:T(4,128)}, u32[]{:S(2)}) copy-start(f32[2,4,128]{2,1,0:T(4,128)} %rest_5_.1) | copy-start | bytes 12292
  44.6 14.5 %copy-start.14 = (f32[2,128,128]{2,1,0:T(8,128)S(1)}, f32[2,128,128]{2,1,0:T(8,128)}, u32[]{:S(2)}) copy-start(f32[2,128,128]{2,1,0:T(8,128)} %wo_ref.3) | copy-start | bytes 393220
  50.3 8.8 %collective-permute-start.10 = (bf16[16,2,48,768]{3,2,1,0:T(8,128)(2,1)S(1)}, bf16[16,2,48,768]{3,2,1,0:T(8,128)(2,1)S(1)}, u32[]{:S(2)}, u32[]{:S(2)}) collective-permute-start(bf16[16,2,48,768]{3,2,1,0:T(8,128)(2,1)S(1)} %pad_maximum_fusion.rest_0_), channel_id=1, source_target_pairs={{0,1},{1,0},{2,3},{3,2},{4,5},{5,4},{6,7},{7,6},{8,9},{9,8},{10,11... | collective-permute-start | bytes 7077896 | tf_op jit(solution)/shard_map/ppermute | solution.py:49
  75.8 1.1 copy-start.3
  76.9 1.2 collective-permute-start.11
  78.1 2.8 %collective-permute-start.14 = (bf16[48,384]{1,0:T(8,128)(2,1)S(1)}, bf16[48,384]{1,0:T(8,128)(2,1)S(1)}, u32[]{:S(2)}, u32[]{:S(2)}) collective-permute-start(bf16[48,384]{1,0:T(8,128)(2,1)S(1)} %constant_dynamic-update-slice_fusion.2.refs_0_), channel_id=1, source_target_pairs={{0,6},{1,7},{2,0},{3,1},{4,2},{5,3},{6,4},{7,5},{8,14},{9,15},{10,... | collective-permute-start | bytes 110600 | tf_op jit(solution)/shard_map/ppermute | solution.py:49
  78.4 4.3 %collective-permute-start.13 = (bf16[48,384]{1,0:T(8,128)(2,1)S(1)}, bf16[48,384]{1,0:T(8,128)(2,1)S(1)}, u32[]{:S(2)}, u32[]{:S(2)}) collective-permute-start(bf16[48,384]{1,0:T(8,128)(2,1)S(1)} %constant_dynamic-update-slice_fusion.2.refs_0_), channel_id=1, source_target_pairs={{0,4},{1,5},{2,6},{3,7},{4,0},{5,1},{6,2},{7,3},{8,12},{9,13},{10,... | collective-permute-start | bytes 110600 | tf_op jit(solution)/shard_map/ppermute | solution.py:49
  79.5 4.6 %collective-permute-start.12 = (bf16[48,384]{1,0:T(8,128)(2,1)S(1)}, bf16[48,384]{1,0:T(8,128)(2,1)S(1)}, u32[]{:S(2)}, u32[]{:S(2)}) collective-permute-start(bf16[48,384]{1,0:T(8,128)(2,1)S(1)} %constant_dynamic-update-slice_fusion.2.refs_0_), channel_id=1, source_target_pairs={{0,2},{1,3},{2,4},{3,5},{4,6},{5,7},{6,0},{7,1},{8,10},{9,11},{10,... | collective-permute-start | bytes 110600 | tf_op jit(solution)/shard_map/ppermute | solution.py:49
  84.1 28.8 %all-to-all-start = ((s16[128,40,128]{2,1,0:T(8,128)(2,1)}), s16[128,40,128]{2,1,0:T(8,128)(2,1)}, u32[]{:S(2)}, u32[]{:S(2)}) async-start(s16[128,40,128]{2,1,0:T(8,128)(2,1)} %bitcast.11), calls=%async_computation | async-start | bytes 2621440 | tf_op jit(solution)/shard_map/all_to_all | solution.py:466
  90.7 17.3 %collective-permute-start.17 = (bf16[1,2,48,768]{3,2,1,0:T(8,128)(2,1)S(1)}, bf16[1,2,48,768]{3,2,1,0:T(8,128)(2,1)S(1)}, u32[]{:S(2)}, u32[]{:S(2)}) collective-permute-start(bf16[1,2,48,768]{3,2,1,0:T(8,128)(2,1)S(1)} %shard_map.113), channel_id=1, source_target_pairs={{0,72},{1,49},{2,74},{3,51},{4,76},{5,53},{6,78},{7,55},{8,64},{9,... | collective-permute-start | bytes 442376 | tf_op jit(solution)/shard_map/ppermute | solution.py:49
  94.2 15.5 %collective-permute-start.16 = (bf16[1,2,48,768]{3,2,1,0:T(8,128)(2,1)S(1)}, bf16[1,2,48,768]{3,2,1,0:T(8,128)(2,1)S(1)}, u32[]{:S(2)}, u32[]{:S(2)}) collective-permute-start(bf16[1,2,48,768]{3,2,1,0:T(8,128)(2,1)S(1)} %shard_map.113), channel_id=1, source_target_pairs={{0,8},{1,33},{2,10},{3,35},{4,12},{5,37},{6,14},{7,39},{8,0},{9,41... | collective-permute-start | bytes 442376 | tf_op jit(solution)/shard_map/ppermute | solution.py:49
  94.3 17.7 %collective-permute-start.15 = (bf16[1,2,48,768]{3,2,1,0:T(8,128)(2,1)S(1)}, bf16[1,2,48,768]{3,2,1,0:T(8,128)(2,1)S(1)}, u32[]{:S(2)}, u32[]{:S(2)}) collective-permute-start(bf16[1,2,48,768]{3,2,1,0:T(8,128)(2,1)S(1)} %shard_map.113), channel_id=1, source_target_pairs={{0,64},{1,17},{2,66},{3,19},{4,68},{5,21},{6,70},{7,23},{8,72},{9,... | collective-permute-start | bytes 442376 | tf_op jit(solution)/shard_map/ppermute | solution.py:49
  112.9 15.7 %collective-permute-start.20 = (bf16[4,2,48,768]{3,2,1,0:T(8,128)(2,1)}, bf16[4,2,48,768]{3,2,1,0:T(8,128)(2,1)S(1)}, u32[]{:S(2)}, u32[]{:S(2)}) collective-permute-start(bf16[4,2,48,768]{3,2,1,0:T(8,128)(2,1)} %pad_maximum_fusion.3), channel_id=1, source_target_pairs={{0,48},{1,73},{2,50},{3,75},{4,52},{5,77},{6,54},{7,79},{8,56},{9,... | collective-permute-start | bytes 1769480 | tf_op jit(solution)/shard_map/ppermute | solution.py:49
  115.1 13.5 %collective-permute-start.19 = (bf16[4,2,48,768]{3,2,1,0:T(8,128)(2,1)}, bf16[4,2,48,768]{3,2,1,0:T(8,128)(2,1)S(1)}, u32[]{:S(2)}, u32[]{:S(2)}) collective-permute-start(bf16[4,2,48,768]{3,2,1,0:T(8,128)(2,1)} %pad_maximum_fusion.3), channel_id=1, source_target_pairs={{0,32},{1,9},{2,34},{3,11},{4,36},{5,13},{6,38},{7,15},{8,40},{9,1... | collective-permute-start | bytes 1769480 | tf_op jit(solution)/shard_map/ppermute | solution.py:49
  115.6 16.6 %collective-permute-start.18 = (bf16[4,2,48,768]{3,2,1,0:T(8,128)(2,1)}, bf16[4,2,48,768]{3,2,1,0:T(8,128)(2,1)S(1)}, u32[]{:S(2)}, u32[]{:S(2)}) collective-permute-start(bf16[4,2,48,768]{3,2,1,0:T(8,128)(2,1)} %pad_maximum_fusion.3), channel_id=1, source_target_pairs={{0,16},{1,65},{2,18},{3,67},{4,20},{5,69},{6,22},{7,71},{8,24},{9,... | collective-permute-start | bytes 1769480 | tf_op jit(solution)/shard_map/ppermute | solution.py:49
  118.1 14.1 %copy-start.16 = (bf16[4,2,48,768]{3,2,1,0:T(8,128)(2,1)S(1)}, bf16[4,2,48,768]{3,2,1,0:T(8,128)(2,1)}, u32[]{:S(2)}) copy-start(bf16[4,2,48,768]{3,2,1,0:T(8,128)(2,1)} %pad_maximum_fusion.3) | copy-start | bytes 1769476
  132.5 4.6 %collective-permute-start.21 = (bf16[16,2,48,768]{3,2,1,0:T(8,128)(2,1)S(1)}, bf16[16,2,48,768]{3,2,1,0:T(8,128)(2,1)S(1)}, u32[]{:S(2)}, u32[]{:S(2)}) collective-permute-start(bf16[16,2,48,768]{3,2,1,0:T(8,128)(2,1)S(1)} %pad_maximum_fusion.1.rest_0_), channel_id=1, source_target_pairs={{0,1},{1,0},{2,3},{3,2},{4,5},{5,4},{6,7},{7,6},{8,9},{9,8},{10,11... | collective-permute-start | bytes 7077896 | tf_op jit(solution)/shard_map/ppermute | solution.py:49
